TPU v7x, 512 devices: a whole 4x8x8 slice. The times are simulated.
512 devices in a mesh: run: 32 (over y_lo, x, core), tp: 16 (over z, y_hi).
Axes of the slice: x: 4, y: 8 (y_hi: 2, y_lo: 4; y = y_hi * 4 + y_lo), z: 8, core: 2. Of those that a mesh axis runs over, the one named last changes fastest.
Arguments:
- tokens: bfloat16 [16384, 4096], P('run', 'tp'), may hold values from -6 to 6
- output_gradient: bfloat16 [16384, 4096], P('run', 'tp'), may hold values from -6 to 6
- frozen_weight: bfloat16 [4096, 4096], P('tp'), may hold values from -0.09375 to 0.09375
- adapter_down: bfloat16 [32, 4096, 128], P('run', 'tp'), may hold values from -4 to 4
- adapter_up: bfloat16 [32, 128, 4096], P('run', None, 'tp'), may hold values from -4 to 4
- down_adam_moments: float32 [32, 2, 4096, 128], P('run', None, 'tp'), as said below
- up_adam_moments: float32 [32, 2, 128, 4096], P('run', None, None, 'tp'), as said below
- feature_factors: float32 [32, 2, 4096], P('run', None, 'tp'), may hold values from 0.003 to 0.3
- rank_factors: float32 [32, 2, 128], P('run'), may hold values from 0.003 to 0.3
- run_adapter_ranks: int32 [16], replicated, may hold values from 16 to 128, as said below
- run_optimizers: int32 [16], replicated, may hold values from 0 to 1, as said below
- run_owner_slots: int32 [16], replicated, may hold values from 0 to 31, as said below
Outputs:
- layer_output: bfloat16 [16384, 4096], P('run', 'tp')
- input_gradient: bfloat16 [16384, 4096], P('run', 'tp')
- new_down: bfloat16 [32, 4096, 128], P('run', 'tp')
- new_up: bfloat16 [32, 128, 4096], P('run', None, 'tp')
- new_adam_down: float32 [32, 2, 4096, 128], P('run', None, 'tp')
- new_adam_up: float32 [32, 2, 128, 4096], P('run', None, None, 'tp')
- new_factor_wide: float32 [32, 2, 4096], P('run', None, 'tp')
- new_factor_rank: float32 [32, 2, 128], P('run')
Inputs may be any that keep to these rules, and one draw needn't show every extreme that they name: `run_adapter_ranks`: some run has rank 128 and some run has rank 16. `run_optimizers`: 0 is Adam, 1 is Adafactor; both occur. `run_owner_slots`: distinct slots; slots 0 and 32 - 1 are always owned; half of the slots are owned by no run. `down_adam_moments`: index 0 holds first moments within -4 to 4, index 1 positive second moments. `up_adam_moments`: index 0 holds first moments within -4 to 4, index 1 positive second moments.
All inputs are finite; a program needn't handle non-finite values.
Results may differ from a plain program's by a relative error of at most 0.02.
Values may be sent and summed in bfloat16 or wider, within the bound.
No kernel may reach another device: no remote copies, remote signals or barrier semaphores. Data moves between devices by JAX's collectives and lax.ppermute only.
A program may use at most 64 MiB of HBM per device.

v0:
```python
import math

import jax
import jax.numpy as jnp
from jax import lax
from jax.sharding import PartitionSpec as P

RANK_MIN = 16


beta_first = 0.9
beta_second = 0.99
adam_rate = 0.05
adam_eps = 1e-08
factor_rate = 0.05
factor_decay = 0.99
adapter_alpha = 0.5


def to_slots(run_owner_slots, blocks, slot_count):
    onehot = (run_owner_slots[None, :] == jnp.arange(slot_count, dtype=jnp.int32)[:, None]).astype(
        blocks.dtype
    )
    return jnp.einsum("or,rkd->okd", onehot, blocks, preferred_element_type=jnp.float32).astype(
        blocks.dtype
    )


def contract_rows(left_side, right_side):
    return lax.dot_general(
        left_side, right_side, (((0,), (0,)), ((), ())), preferred_element_type=jnp.float32
    )


def contract_last(left_side, right_side):
    return lax.dot_general(
        left_side, right_side, (((1,), (1,)), ((), ())), preferred_element_type=jnp.float32
    )


def adam_step(weights, moments, gradient, keep_mask):
    first_new = beta_first * moments[0] + (1.0 - beta_first) * gradient
    second_new = beta_second * moments[1] + (1.0 - beta_second) * gradient * gradient
    updated = weights.astype(jnp.float32) - adam_rate * first_new / (
        jnp.sqrt(second_new) + adam_eps
    )
    return (updated * keep_mask, jnp.stack([first_new * keep_mask, second_new * keep_mask]))


def local(
    tokens,
    output_gradient,
    frozen_weight,
    adapter_down,
    adapter_up,
    down_adam_moments,
    up_adam_moments,
    feature_factors,
    rank_factors,
    run_adapter_ranks,
    run_optimizers,
    run_owner_slots,
):
    slot_count = lax.axis_size("run")
    token_rows, feature_width = tokens.shape
    full_width = frozen_weight.shape[1]
    rank_extent = adapter_down.shape[2]
    run_count = run_adapter_ranks.shape[0]
    run_rows = token_rows // run_count
    inverse_root = 1.0 / math.sqrt(full_width)
    base_term = jnp.dot(tokens, frozen_weight, preferred_element_type=jnp.float32)
    frozen_total = lax.psum_scatter(
        base_term.astype(jnp.bfloat16), "tp", scatter_dimension=1, tiled=True
    ).astype(jnp.float32)
    backward_total = contract_last(
        lax.all_gather(output_gradient, "tp", axis=1, tiled=True), frozen_weight
    )
    columns = jnp.arange(rank_extent, dtype=jnp.int32)
    position = lax.axis_index("run")
    owned_runs = run_owner_slots == position
    holds_run = jnp.any(owned_runs)
    rank_self = jnp.max(jnp.where(owned_runs, run_adapter_ranks, RANK_MIN))
    kind_self = jnp.max(jnp.where(owned_runs, run_optimizers, 0))
    rank_as_float = rank_self.astype(jnp.float32)
    own_scale = adapter_alpha / jnp.sqrt(rank_as_float)
    keep_self = (columns < rank_self).astype(jnp.float32)
    own_down_map = adapter_down[0]
    own_up_map = adapter_up[0]
    token_runs = tokens.reshape(run_count, run_rows, feature_width)
    grad_runs = output_gradient.reshape(run_count, run_rows, feature_width)
    all_down, all_up = (
        lax.all_gather(adapter_down, "run", axis=0, tiled=True),
        lax.all_gather(adapter_up, "run", axis=0, tiled=True),
    )
    selected_down = jnp.take(all_down, run_owner_slots, axis=0)
    selected_up = jnp.take(all_up, run_owner_slots, axis=0)
    run_scaling = adapter_alpha / jnp.sqrt(run_adapter_ranks.astype(jnp.float32))
    run_mask = (columns[None, :] < run_adapter_ranks[:, None]).astype(jnp.float32)[:, None, :]
    low_part = jnp.einsum(
        "rkd,rdq->rkq", token_runs, selected_down, preferred_element_type=jnp.float32
    )
    back_part = jnp.einsum(
        "rkd,rqd->rkq", grad_runs, selected_up, preferred_element_type=jnp.float32
    )
    low_sum, back_sum = (
        lax.psum(low_part.astype(jnp.bfloat16), "tp").astype(jnp.float32),
        lax.psum(back_part.astype(jnp.bfloat16), "tp").astype(jnp.float32),
    )
    low_rows = (low_sum * inverse_root * run_mask).astype(jnp.bfloat16)
    back_rows = (back_sum * run_mask).astype(jnp.bfloat16)
    adapter_output = run_scaling[:, None, None] * jnp.einsum(
        "rkq,rqd->rkd", low_rows, selected_up, preferred_element_type=jnp.float32
    )
    adapter_backward = (run_scaling * inverse_root)[:, None, None] * jnp.einsum(
        "rkq,rdq->rkd", back_rows, selected_down, preferred_element_type=jnp.float32
    )
    recv_tok, recv_grad, recv_low, recv_back = (
        lax.all_to_all(
            to_slots(run_owner_slots, token_runs, slot_count),
            "run",
            split_axis=0,
            concat_axis=0,
            tiled=True,
        ),
        lax.all_to_all(
            to_slots(run_owner_slots, grad_runs, slot_count),
            "run",
            split_axis=0,
            concat_axis=0,
            tiled=True,
        ),
        lax.all_to_all(
            to_slots(run_owner_slots, low_rows, slot_count),
            "run",
            split_axis=0,
            concat_axis=0,
            tiled=True,
        ),
        lax.all_to_all(
            to_slots(run_owner_slots, back_rows, slot_count),
            "run",
            split_axis=0,
            concat_axis=0,
            tiled=True,
        ),
    )
    flat_low = recv_low.reshape(-1, rank_extent)
    flat_back = recv_back.reshape(-1, rank_extent)
    adapter_output = adapter_output.reshape(token_rows, feature_width)
    adapter_backward = adapter_backward.reshape(token_rows, feature_width)
    layer_output = (frozen_total + adapter_output).astype(jnp.bfloat16)
    input_gradient = (backward_total + adapter_backward).astype(jnp.bfloat16)
    flat_tok = recv_tok.reshape(-1, feature_width)
    flat_grad = recv_grad.reshape(-1, feature_width)
    grad_up = own_scale * contract_rows(flat_low, flat_grad)
    grad_down = own_scale * inverse_root * contract_rows(flat_tok, flat_back)
    keep_down = keep_self[None, :]
    keep_up = keep_self[:, None]
    adam_new_down, moments_down = adam_step(
        own_down_map, down_adam_moments[0], grad_down, keep_down
    )
    adam_new_up, moments_up = adam_step(own_up_map, up_adam_moments[0], grad_up, keep_up)
    square_down = grad_down * grad_down
    square_up = grad_up * grad_up
    row_new_down = (
        factor_decay * feature_factors[0, 0]
        + (1.0 - factor_decay) * jnp.sum(square_down, axis=1) / rank_as_float
    )
    col_new_up = (
        factor_decay * feature_factors[0, 1]
        + (1.0 - factor_decay) * jnp.sum(square_up, axis=0) / rank_as_float
    )
    col_part = jnp.sum(square_down, axis=0)
    row_part = jnp.sum(square_up, axis=1)
    total_part = jnp.sum(row_new_down)
    col_sum, row_sum, row_total = lax.psum((col_part, row_part, total_part), "tp")
    col_new_down = (
        factor_decay * rank_factors[0, 0] + (1.0 - factor_decay) * col_sum / full_width
    ) * keep_self
    row_new_up = (
        factor_decay * rank_factors[0, 1] + (1.0 - factor_decay) * row_sum / full_width
    ) * keep_self
    mean_down = row_total / full_width
    mean_up = jnp.sum(row_new_up) / rank_as_float
    col_safe = jnp.where(keep_self > 0, col_new_down, 1.0)
    row_safe = jnp.where(keep_self > 0, row_new_up, 1.0)
    step_down = grad_down * jnp.sqrt(mean_down / (row_new_down[:, None] * col_safe[None, :]))
    step_up = grad_up * jnp.sqrt(mean_up / (row_safe[:, None] * col_new_up[None, :]))
    fact_down = (own_down_map.astype(jnp.float32) - factor_rate * step_down) * keep_down
    fact_up = (own_up_map.astype(jnp.float32) - factor_rate * step_up) * keep_up
    is_adam = kind_self == 0
    new_down = jnp.where(holds_run, jnp.where(is_adam, adam_new_down, fact_down), 0.0).astype(
        jnp.bfloat16
    )[None]
    new_up = jnp.where(holds_run, jnp.where(is_adam, adam_new_up, fact_up), 0.0).astype(
        jnp.bfloat16
    )[None]
    new_adam_down = jnp.where(
        holds_run, jnp.where(is_adam, moments_down, down_adam_moments[0]), 0.0
    )[None]
    new_adam_up = jnp.where(holds_run, jnp.where(is_adam, moments_up, up_adam_moments[0]), 0.0)[
        None
    ]
    new_factor_wide = jnp.where(
        holds_run,
        jnp.where(is_adam, feature_factors[0], jnp.stack([row_new_down, col_new_up])),
        0.0,
    )[None]
    new_factor_rank = jnp.where(
        holds_run, jnp.where(is_adam, rank_factors[0], jnp.stack([col_new_down, row_new_up])), 0.0
    )[None]
    return (
        layer_output,
        input_gradient,
        new_down,
        new_up,
        new_adam_down,
        new_adam_up,
        new_factor_wide,
        new_factor_rank,
    )


def solution(mesh):
    placed = (
        P("run", "tp"),
        P("run", "tp"),
        P("tp", None),
        P("run", "tp", None),
        P("run", None, "tp"),
        P("run", None, "tp", None),
        P("run", None, None, "tp"),
        P("run", None, "tp"),
        P("run", None, None),
        P(),
        P(),
        P(),
    )
    return jax.shard_map(
        local,
        mesh=mesh,
        in_specs=placed,
        out_specs=(
            P("run", "tp"),
            P("run", "tp"),
            P("run", "tp", None),
            P("run", None, "tp"),
            P("run", None, "tp", None),
            P("run", None, None, "tp"),
            P("run", None, "tp"),
            P("run", None, None),
        ),
        check_vma=False,
    )
```

profile of v0, /device:TPU:56, one launch (start us, length us, event | category | flops | bytes accessed | tf_op | source)
XLA Modules:
  0.0 726.5 jit_solution(15301666929155902224)
XLA Ops:
  7.2 0.0 copy-start
  7.2 0.0 all-gather.4.cloned.1.call-start
  7.2 0.7 all-gather.4.cloned.1.call-update
  7.9 0.0 all-gather.6.cloned.1.call-start
  8.0 0.7 all-gather.6.cloned.1.call-update
  8.7 0.0 all-reduce.4.cloned.1.call-start
  8.7 1.3 select_reduce_fusion.1
  10.1 1.3 fusion.52
  11.4 65.5 %all-gather.4.cloned.1.call-done = bf16[32,256,128]{2,1,0:T(8,128)(2,1)} async-done(((bf16[1,256,128]{2,1,0:T(8,128)(2,1)}), bf16[32,256,128]{2,1,0:T(8,128)(2,1)}) %all-gather.4.cloned.1.call-update) | async-done | bytes 2097168 | tf_op jit(solution)/shard_map/all_gather | solution.py:92
  76.9 2.3 gather_fusion
  79.2 1.1 fusion.2
  80.3 60.6 %all-gather.6.cloned.1.call-done = bf16[32,128,256]{2,1,0:T(8,128)(2,1)} async-done(((bf16[1,128,256]{2,1,0:T(8,128)(2,1)}), bf16[32,128,256]{2,1,0:T(8,128)(2,1)}) %all-gather.6.cloned.1.call-update) | async-done | bytes 2097168 | tf_op jit(solution)/shard_map/all_gather | solution.py:93
  140.9 3.2 gather_fusion.1
  144.0 2.5 fusion.1
  146.5 0.0 all-reduce.4.cloned.1.call-update
  146.5 0.0 all-gather.8.cloned.1.call-start
  146.6 0.5 all-gather.8.cloned.1.call-update
  147.1 0.0 reduce-scatter.2.cloned.1.call-start
  147.2 3.2 convolution_convert_fusion
  150.4 0.0 reduce-scatter.2.cloned.1.call-update
  150.4 0.6 copy-done.10
  151.0 0.3 fusion.10
  151.3 0.0 copy-start.11
  151.3 1.1 copy.41
  152.4 6.8 all-to-all-start
  159.9 0.3 fusion.8
  160.2 1.1 copy.40
  162.0 0.6 slice_multiply_fusion
  162.6 11.3 %all-to-all-done = bf16[32,32,256]{2,1,0:T(8,128)(2,1)S(1)} async-done(((bf16[32,32,256]{2,1,0:T(8,128)(2,1)}), bf16[32,32,256]{2,1,0:T(8,128)(2,1)S(1)}, u32[]{:S(2)}, u32[]{:S(2)}) %all-to-all-start) | async-done | bytes 524320 | tf_op jit(solution)/shard_map/all_to_all | solution.py:118
  173.9 0.8 copy-done.7
  174.7 7.5 %all-to-all-start.3 = ((bf16[32,32,256]{2,1,0:T(8,128)(2,1)}), bf16[32,32,256]{2,1,0:T(8,128)(2,1)S(1)}, u32[]{:S(2)}, u32[]{:S(2)}) async-start(bf16[32,32,256]{2,1,0:T(8,128)(2,1)} %copy.40), calls=%async_computation.4 | async-start | bytes 1048576 | tf_op jit(solution)/shard_map/all_to_all | solution.py:125
  182.2 1.2 fusion.45
  183.4 0.1 fusion.40
  183.4 0.1 fusion.39
  183.5 160.7 %all-reduce.4.cloned.1.call-done = (bf16[16,32,128]{2,1,0:T(8,128)(2,1)}, bf16[16,32,128]{2,1,0:T(8,128)(2,1)}) async-done(((bf16[16,32,128]{2,1,0:T(8,128)(2,1)}, bf16[16,32,128]{2,1,0:T(8,128)(2,1)}), (bf16[16,32,128]{2,1,0:T(8,128)(2,1)}, bf16[16,32,128]{2,1,0:T(8,128)(2,1)})) %all-reduce.4.cloned.1.call-update) | async-done | bytes 262160 | tf_op jit(solution)/shard_map/psum | solution.py:106
  344.2 0.9 multiply_convert_fusion
  345.1 0.2 fusion.26
  345.3 0.8 copy.43
  346.1 7.7 %all-to-all-start.1 = ((bf16[32,32,128]{2,1,0:T(8,128)(2,1)}), bf16[32,32,128]{2,1,0:T(8,128)(2,1)S(1)}, u32[]{:S(2)}, u32[]{:S(2)}) async-start(bf16[32,32,128]{2,1,0:T(8,128)(2,1)} %copy.43), calls=%async_computation.2 | async-start | bytes 524288 | tf_op jit(solution)/shard_map/all_to_all | solution.py:139
  353.9 0.9 multiply_convert_fusion.1
  354.8 0.2 fusion.24
  355.0 0.8 copy.42
  355.9 2.4 convolution_multiply_fusion.1
  358.2 4.3 all-to-all-done.1
  362.5 6.3 all-to-all-start.2
  368.9 2.6 convolution_multiply_fusion
  371.5 2.7 multiply_reduce_fusion.3
  374.2 0.6 fusion.57
  374.8 2.9 all-to-all-done.2
  377.7 0.9 multiply_reduce_fusion.1
  378.6 51.4 %all-reduce = (f32[128]{0:T(128)S(1)}, f32[]{:T(128)}, f32[128]{0:T(128)S(1)}) all-reduce(f32[128]{0:T(128)} %get-tuple-element.11, f32[]{:T(128)} %get-tuple-element.25, f32[128]{0:T(128)} %get-tuple-element.8), channel_id=1, replica_groups=mesh['run'=32,'tp'=16] {'tp'}, use_global_device_ids=true, to_apply=%region_10.11 | all-reduce | flops 257 | bytes 2056 | tf_op jit(solution)/shard_map/psum | solution.py:176
  430.0 2.0 fusion.53
  433.3 0.7 compare_select_fusion.1
  434.0 1.9 fusion.42
  435.9 0.7 fusion.55
  436.6 1.2 fusion.41
  437.8 2.4 multiply_bitcast_fusion.3
  440.2 1.4 fusion.6
  441.6 2.3 multiply_bitcast_fusion.1
  443.9 1.4 fusion.7
  445.3 33.1 %all-gather.8.cloned.1.call-done = bf16[512,4096]{1,0:T(8,128)(2,1)} async-done(((bf16[512,256]{1,0:T(8,128)(2,1)}), bf16[512,4096]{1,0:T(8,128)(2,1)}) %all-gather.8.cloned.1.call-update) | async-done | bytes 4194320 | tf_op jit(solution)/shard_map/all_gather | solution.py:76
  478.4 4.3 fusion
  482.8 235.5 %reduce-scatter.2.cloned.1.call-done = bf16[512,256]{1,0:T(8,128)(2,1)} async-done(((bf16[512,4096]{1,0:T(8,128)(2,1)}), bf16[512,256]{1,0:T(8,128)(2,1)}) %reduce-scatter.2.cloned.1.call-update) | async-done | bytes 262160 | tf_op jit(solution)/shard_map/reduce_scatter | solution.py:72
  718.3 1.7 fusion.5
  (24 shorter events, 0.1 us)
Async XLA Ops:
  7.2 140.0 %copy-start = (bf16[256,4096]{1,0:T(8,128)(2,1)S(1)}, bf16[256,4096]{1,0:T(8,128)(2,1)}, u32[]{:S(2)}) copy-start(bf16[256,4096]{1,0:T(8,128)(2,1)} %param.14) | copy-start | bytes 6291460
  7.2 72.0 %copy-start.2 = (bf16[512,256]{1,0:T(8,128)(2,1)S(1)}, bf16[512,256]{1,0:T(8,128)(2,1)}, u32[]{:S(2)}) copy-start(bf16[512,256]{1,0:T(8,128)(2,1)} %param.12) | copy-start | bytes 786436
  7.2 69.7 %all-gather.4.cloned.1.call-start = ((), (), s32[]{:S(2)}) async-start(), calls=%async_computation.6 | async-start | bytes 2162688 | tf_op jit(solution)/shard_map/all_gather | solution.py:92
  7.9 133.0 %all-gather.6.cloned.1.call-start = ((), (), s32[]{:S(2)}) async-start(), calls=%async_computation.7 | async-start | bytes 2162688 | tf_op jit(solution)/shard_map/all_gather | solution.py:93
  8.7 335.5 %all-reduce.4.cloned.1.call-start = ((), (), s32[]{:S(2)}) async-start(), calls=%async_computation.9 | async-start | bytes 524288 | tf_op jit(solution)/shard_map/psum | solution.py:106
  79.2 67.3 %copy-start.1 = (bf16[16,256,128]{2,1,0:T(8,128)(2,1)}, bf16[16,256,128]{2,1,0:T(8,128)(2,1)S(1)}, u32[]{:S(2)}) copy-start(bf16[16,256,128]{2,1,0:T(8,128)(2,1)S(1)} %gather_fusion) | copy-start | bytes 3145732
  146.5 331.9 %all-gather.8.cloned.1.call-start = ((), (), s32[]{:S(2)}) async-start(), calls=%async_computation.8 | async-start | bytes 4456448 | tf_op jit(solution)/shard_map/all_gather | solution.py:76
  147.1 571.2 %reduce-scatter.2.cloned.1.call-start = ((), (), s32[]{:S(2)}) async-start(), calls=%async_computation.5 | async-start | bytes 4456448 | tf_op jit(solution)/shard_map/reduce_scatter | solution.py:72
  150.4 0.7 copy-start.10
  151.0 8.9 %copy-start.5 = (bf16[512,256]{1,0:T(8,128)(2,1)S(1)}, bf16[512,256]{1,0:T(8,128)(2,1)}, u32[]{:S(2)}) copy-start(bf16[512,256]{1,0:T(8,128)(2,1)} %param.13) | copy-start | bytes 786436
  151.3 10.7 %copy-start.11 = (s32[16]{0:T(128)S(1)}, s32[16]{0:T(128)}, u32[]{:S(2)}) copy-start(s32[16]{0:T(128)} %param.21) | copy-start | bytes 196
  151.3 10.7 %copy-start.9 = (f32[1,2,256]{2,1,0:T(2,128)S(1)}, f32[1,2,256]{2,1,0:T(2,128)}, u32[]{:S(2)}) copy-start(f32[1,2,256]{2,1,0:T(2,128)} %param.19) | copy-start | bytes 6148
  152.4 21.5 %all-to-all-start = ((bf16[32,32,256]{2,1,0:T(8,128)(2,1)}), bf16[32,32,256]{2,1,0:T(8,128)(2,1)S(1)}, u32[]{:S(2)}, u32[]{:S(2)}) async-start(bf16[32,32,256]{2,1,0:T(8,128)(2,1)} %copy.41), calls=%async_computation.1 | async-start | bytes 1048576 | tf_op jit(solution)/shard_map/all_to_all | solution.py:118
  173.9 0.8 copy-start.7
  174.7 171.5 %all-to-all-start.3 = ((bf16[32,32,256]{2,1,0:T(8,128)(2,1)}), bf16[32,32,256]{2,1,0:T(8,128)(2,1)S(1)}, u32[]{:S(2)}, u32[]{:S(2)}) async-start(bf16[32,32,256]{2,1,0:T(8,128)(2,1)} %copy.40), calls=%async_computation.4 | async-start | bytes 1048576 | tf_op jit(solution)/shard_map/all_to_all | solution.py:125
  346.1 16.4 %all-to-all-start.1 = ((bf16[32,32,128]{2,1,0:T(8,128)(2,1)}), bf16[32,32,128]{2,1,0:T(8,128)(2,1)S(1)}, u32[]{:S(2)}, u32[]{:S(2)}) async-start(bf16[32,32,128]{2,1,0:T(8,128)(2,1)} %copy.43), calls=%async_computation.2 | async-start | bytes 524288 | tf_op jit(solution)/shard_map/all_to_all | solution.py:139
  362.5 6.4 copy-start.8
  362.5 15.2 %all-to-all-start.2 = ((bf16[32,32,128]{2,1,0:T(8,128)(2,1)}), bf16[32,32,128]{2,1,0:T(8,128)(2,1)S(1)}, u32[]{:S(2)}, u32[]{:S(2)}) async-start(bf16[32,32,128]{2,1,0:T(8,128)(2,1)} %copy.42), calls=%async_computation.3 | async-start | bytes 524288 | tf_op jit(solution)/shard_map/all_to_all | solution.py:132
  368.9 68.9 %copy-start.3 = (f32[1,2,256,128]{3,2,1,0:T(8,128)S(1)}, f32[1,2,256,128]{3,2,1,0:T(8,128)}, u32[]{:S(2)}) copy-start(f32[1,2,256,128]{3,2,1,0:T(8,128)} %param.17) | copy-start | bytes 786436
  371.5 70.0 %copy-start.4 = (f32[1,2,128,256]{3,2,1,0:T(8,128)S(1)}, f32[1,2,128,256]{3,2,1,0:T(8,128)}, u32[]{:S(2)}) copy-start(f32[1,2,128,256]{3,2,1,0:T(8,128)} %param.18) | copy-start | bytes 786436
  478.4 239.8 %copy-start.6 = (f32[16,32,256]{2,1,0:T(8,128)S(1)}, f32[16,32,256]{2,1,0:T(8,128)}, u32[]{:S(2)}) copy-start(f32[16,32,256]{2,1,0:T(8,128)} %convolution_multiply_fusion.1) | copy-start | bytes 1572868
Sparse Core Ops, SparseCore 0:
  10.2 66.6 all-gather.3
  79.0 61.8 all-gather.5
  146.6 197.4 all-reduce.3
  347.5 130.8 all-gather.7
  483.6 234.6 reduce-scatter.1
where the time goes:
time: 732 us; the launch traced here: 727 us
  waiting for transfers between devices  576 us (79%)
  blocking collectives  51.4 us (7%)
  starting transfers between devices  28.6 us (4%)
  other arithmetic  22.7 us (3%)
  matrix products  20.6 us (3%)
  between operations  16.6 us (2%)
  local copies, waits for them, and re-layouts  10.8 us (1%)
    reduce_scatter x1, waiting for transfers between devices, local(): lax.psum_scatter(base_term.astype(jnp.bfloat16), 'tp', scatter_dimension=...  235 us
    psum x1, waiting for transfers between devices, local(): lax.psum(low_part.astype(jnp.bfloat16), 'tp').astype(jnp.float32)  161 us
    all_gather x1, waiting for transfers between devices, local(): lax.all_gather(adapter_down, 'run', axis=0, tiled=True)  65.5 us
    all_gather x1, waiting for transfers between devices, local(): lax.all_gather(adapter_up, 'run', axis=0, tiled=True)  60.6 us
    psum x1, blocking collectives, local(): lax.psum((col_part, row_part, total_part), 'tp')  51.4 us
    all_gather x1, waiting for transfers between devices, local(): lax.all_gather(output_gradient, 'tp', axis=1, tiled=True)  33.1 us
  transfers between devices with their start and end apart: 9, of which 8 were waited for; matrix products, arithmetic and copies ran while one was open for 6% of the time, Pallas kernels for 0%

commit v1 on v0

v1 whole, which is shorter than its diff:
```python
import functools
import math

import jax
import jax.numpy as jnp
from jax import lax
from jax.experimental import pallas as pl
from jax.experimental.pallas import tpu as pltpu
from jax.sharding import PartitionSpec as P

RANK_MIN = 16

beta_first = 0.9
beta_second = 0.99
adam_rate = 0.05
adam_eps = 1e-08
factor_rate = 0.05
factor_decay = 0.99
adapter_alpha = 0.5

F32 = jnp.float32
BF16 = jnp.bfloat16
SMEM = pl.BlockSpec(memory_space=pltpu.SMEM)
PARAMS = pltpu.CompilerParams(vmem_limit_bytes=60 * 1024 * 1024)


def shape(dims, dtype):
    return jax.ShapeDtypeStruct(dims, dtype)


def whole(dims, index=None):
    if index is None:
        return pl.BlockSpec(dims, lambda step: (0,) * len(dims))
    return pl.BlockSpec((None,) + dims[1:], lambda step: (index,) + (0,) * (len(dims) - 1))


def staged_call(body, out_shape, scalars, operands, after=()):
    used, extra = len(scalars) + len(operands), len(after)
    pairs = [operand if isinstance(operand, tuple) else (operand, None) for operand in operands]

    def without_extra(*refs):
        body(*refs[:used], *refs[used + extra :])

    return pl.pallas_call(
        without_extra,
        out_shape=out_shape,
        grid=(1,),
        in_specs=[SMEM] * len(scalars)
        + [whole(operand.shape, index) for operand, index in pairs]
        + [pl.BlockSpec(memory_space=pl.ANY)] * extra,
        out_specs=tuple(whole(out.shape) for out in out_shape),
        compiler_params=PARAMS,
    )(*scalars, *[operand for operand, _ in pairs], *after)


def contract(left_side, right_side, left_dim, right_dim):
    return lax.dot_general(
        left_side,
        right_side,
        (((left_dim,), (right_dim,)), ((), ())),
        preferred_element_type=F32,
    )


def all_to_all(blocks, axis):
    return lax.all_to_all(blocks, axis, split_axis=0, concat_axis=0, tiled=True)


def to_column(row):
    extent = row.shape[1]
    eye = lax.broadcasted_iota(jnp.int32, (extent, extent), 0) == lax.broadcasted_iota(
        jnp.int32, (extent, extent), 1
    )
    return jnp.sum(jnp.where(eye, row, 0.0), axis=1, keepdims=True)


def to_row(column):
    extent = column.shape[0]
    eye = lax.broadcasted_iota(jnp.int32, (extent, extent), 0) == lax.broadcasted_iota(
        jnp.int32, (extent, extent), 1
    )
    return jnp.sum(jnp.where(eye, column, 0.0), axis=0, keepdims=True)


def own_run(place_ref, slots_ref, ranks_ref, kinds_ref):
    rank, kind, holds = jnp.int32(RANK_MIN), jnp.int32(0), jnp.int32(0)
    for run in range(slots_ref.shape[0]):
        owned = slots_ref[run] == place_ref[0]
        rank = jnp.where(owned, ranks_ref[run], rank)
        kind = jnp.where(owned, kinds_ref[run], kind)
        holds = jnp.where(owned, 1, holds)
    return rank, kind, holds


def scatter_kernel(slots_ref, tok_ref, grad_ref, out_ref):
    run_count = slots_ref.shape[0]
    rows = tok_ref.shape[0] // run_count
    out_ref[...] = jnp.zeros_like(out_ref)
    for run in range(run_count):
        slot = slots_ref[run]
        out_ref[slot, :rows, :] = tok_ref[run * rows : (run + 1) * rows, :]
        out_ref[slot, rows:, :] = grad_ref[run * rows : (run + 1) * rows, :]


def partial_kernel(place_ref, tok_ref, weight_ref, after_ref, out_ref):
    width = out_ref.shape[3]
    product = jnp.dot(tok_ref[...], weight_ref[...], preferred_element_type=F32)
    for part in range(out_ref.shape[1]):
        out_ref[0, part] = product[:, part * width : (part + 1) * width].astype(out_ref.dtype)


def backward_kernel(place_ref, own_ref, other_ref, weight_ref, out_ref):
    width = out_ref.shape[1]
    half = place_ref[1]
    first = pl.ds(pl.multiple_of(half * width, width), width)
    second = pl.ds(pl.multiple_of((1 - half) * width, width), width)

    @pl.when(pl.program_id(0) == 0)
    def _():
        out_ref[...] = jnp.zeros_like(out_ref)

    out_ref[...] += contract(own_ref[0], weight_ref[:, first], 1, 1) + contract(
        other_ref[0], weight_ref[:, second], 1, 1
    )


def low_kernel(recv_ref, down_ref, up_ref, out_ref):
    slots, both_rows, width = recv_ref.shape
    rows = both_rows // 2
    rank = down_ref.shape[2]
    tok = recv_ref[:, :rows, :].reshape(slots * rows, width)
    grad = recv_ref[:, rows:, :].reshape(slots * rows, width)
    low = contract(tok, down_ref[0], 1, 0).astype(out_ref.dtype)
    back = contract(grad, up_ref[0], 1, 1).astype(out_ref.dtype)
    blocks, block_rows, _ = out_ref.shape
    out_ref[:, :, :rank] = low.reshape(blocks, block_rows, rank)
    out_ref[:, :, rank:] = back.reshape(blocks, block_rows, rank)


def reduce_kernel(inverse_root, place_ref, slots_ref, ranks_ref, kinds_ref, part_ref, out_ref):
    rank, _, _ = own_run(place_ref, slots_ref, ranks_ref, kinds_ref)
    extent = part_ref.shape[2] // 2
    column = lax.broadcasted_iota(jnp.int32, (1, 2 * extent), 1)
    keep = (jnp.where(column < extent, column, column - extent) < rank).astype(F32)
    factor = keep * jnp.where(column < extent, F32(inverse_root), F32(1.0))
    total = part_ref[0].astype(F32)
    for block in range(1, part_ref.shape[0]):
        total += part_ref[block].astype(F32)
    rounded = (total * factor).astype(out_ref.dtype)
    for block in range(out_ref.shape[0]):
        out_ref[block] = rounded


def scale_row(rank, extent):
    return adapter_alpha / jnp.sqrt(jnp.full((1, extent), rank, jnp.int32).astype(F32))


def home_kernel(
    inverse_root, place_ref, slots_ref, ranks_ref, kinds_ref, low_ref, down_ref, up_ref, out_ref
):
    rank, _, _ = own_run(place_ref, slots_ref, ranks_ref, kinds_ref)
    slots, both_rows, width = out_ref.shape
    rows = both_rows // 2
    extent = down_ref.shape[2]
    scale = scale_row(rank, width)
    low = low_ref[:, :, :extent].reshape(slots * rows, extent)
    back = low_ref[:, :, extent:].reshape(slots * rows, extent)
    forward = scale * contract(low, up_ref[0], 1, 0)
    backward = (scale * inverse_root) * contract(back, down_ref[0], 1, 1)
    out_ref[:, :rows, :] = forward.astype(out_ref.dtype).reshape(slots, rows, width)
    out_ref[:, rows:, :] = backward.astype(out_ref.dtype).reshape(slots, rows, width)


def grad_kernel(
    inverse_root,
    place_ref,
    slots_ref,
    ranks_ref,
    kinds_ref,
    recv_ref,
    low_ref,
    wide_ref,
    down_ref,
    up_ref,
    wide_new_ref,
    sums_ref,
):
    rank, _, _ = own_run(place_ref, slots_ref, ranks_ref, kinds_ref)
    slots, both_rows, width = recv_ref.shape
    rows = both_rows // 2
    extent = low_ref.shape[2] // 2
    tok = recv_ref[:, :rows, :].reshape(slots * rows, width)
    grad = recv_ref[:, rows:, :].reshape(slots * rows, width)
    low = low_ref[:, :, :extent].reshape(slots * rows, extent)
    back = low_ref[:, :, extent:].reshape(slots * rows, extent)
    grad_up = scale_row(rank, width) * contract(low, grad, 0, 0)
    grad_down = (scale_row(rank, extent) * inverse_root) * contract(tok, back, 0, 0)
    up_ref[...] = grad_up
    down_ref[...] = grad_down
    square_up = grad_up * grad_up
    square_down = grad_down * grad_down
    rank_row = jnp.full((1, width), rank, jnp.int32).astype(F32)
    row_new = (
        factor_decay * wide_ref[0, 0:1, :]
        + (1.0 - factor_decay) * to_row(jnp.sum(square_down, axis=1, keepdims=True)) / rank_row
    )
    col_new = (
        factor_decay * wide_ref[0, 1:2, :]
        + (1.0 - factor_decay) * jnp.sum(square_up, axis=0, keepdims=True) / rank_row
    )
    wide_new_ref[0, 0:1, :] = row_new
    wide_new_ref[0, 1:2, :] = col_new
    col_part = jnp.sum(square_down, axis=0, keepdims=True)
    row_part = to_row(jnp.sum(square_up, axis=1, keepdims=True))
    total = jnp.broadcast_to(jnp.sum(row_new, axis=1, keepdims=True), (1, extent))
    sums = jnp.concatenate(
        [col_part, row_part, total, jnp.zeros((sums_ref.shape[0] - 3, extent), F32)], axis=0
    )
    sums_ref[...] = sums


def update_kernel(
    full_width,
    place_ref,
    slots_ref,
    ranks_ref,
    kinds_ref,
    grad_down_ref,
    grad_up_ref,
    wide_new_ref,
    sums_ref,
    down_ref,
    up_ref,
    down_moments_ref,
    up_moments_ref,
    wide_ref,
    rank_ref,
    new_down_ref,
    new_up_ref,
    new_down_moments_ref,
    new_up_moments_ref,
    new_wide_ref,
    new_rank_ref,
):
    rank, kind, holds = own_run(place_ref, slots_ref, ranks_ref, kinds_ref)
    extent = sums_ref.shape[1]
    is_adam = kind == 0
    held = holds == 1
    keep_row = (lax.broadcasted_iota(jnp.int32, (1, extent), 1) < rank).astype(F32)
    keep_column = (lax.broadcasted_iota(jnp.int32, (extent, 1), 0) < rank).astype(F32)
    rank_row = jnp.full((1, extent), rank, jnp.int32).astype(F32)
    sums = sums_ref[...]
    col_new = (
        factor_decay * rank_ref[0, 0:1, :] + (1.0 - factor_decay) * sums[0:1, :] / full_width
    ) * keep_row
    row_new = (
        factor_decay * rank_ref[0, 1:2, :] + (1.0 - factor_decay) * sums[1:2, :] / full_width
    ) * keep_row
    mean_down = sums[2:3, :] / full_width
    mean_up = jnp.sum(row_new, axis=1, keepdims=True) / rank_row
    col_safe = jnp.where(keep_row > 0, col_new, 1.0)
    row_safe = to_column(jnp.where(keep_row > 0, row_new, 1.0))
    wide_row = wide_new_ref[0, 0:1, :]
    wide_col = wide_new_ref[0, 1:2, :]

    def adam(weights, moments_ref, gradient):
        first = beta_first * moments_ref[0, 0] + (1.0 - beta_first) * gradient
        second = beta_second * moments_ref[0, 1] + (1.0 - beta_second) * gradient * gradient
        return weights - adam_rate * first / (jnp.sqrt(second) + adam_eps), first, second

    def finish(weights_ref, moments_ref, gradient, step, keep, new_ref, new_moments_ref):
        weights = weights_ref[0].astype(F32)
        updated, first, second = adam(weights, moments_ref, gradient)
        factored = weights - factor_rate * step
        value = jnp.where(is_adam, updated, factored) * keep
        new_ref[0] = jnp.where(held, value, 0.0).astype(new_ref.dtype)
        new_moments_ref[0, 0] = jnp.where(
            held, jnp.where(is_adam, first * keep, moments_ref[0, 0]), 0.0
        )
        new_moments_ref[0, 1] = jnp.where(
            held, jnp.where(is_adam, second * keep, moments_ref[0, 1]), 0.0
        )

    grad_down = grad_down_ref[...]
    step_down = grad_down * jnp.sqrt(mean_down / (to_column(wide_row) * col_safe))
    finish(
        down_ref,
        down_moments_ref,
        grad_down,
        step_down,
        keep_row,
        new_down_ref,
        new_down_moments_ref,
    )
    grad_up = grad_up_ref[...]
    step_up = grad_up * jnp.sqrt(mean_up[:, :1] / (row_safe * wide_col))
    finish(
        up_ref, up_moments_ref, grad_up, step_up, keep_column, new_up_ref, new_up_moments_ref
    )
    new_wide_ref[0] = jnp.where(held, jnp.where(is_adam, wide_ref[0], wide_new_ref[0]), 0.0)
    new_rank_ref[0, 0:1, :] = jnp.where(
        held, jnp.where(is_adam, rank_ref[0, 0:1, :], col_new), 0.0
    )
    new_rank_ref[0, 1:2, :] = jnp.where(
        held, jnp.where(is_adam, rank_ref[0, 1:2, :], row_new), 0.0
    )


def output_kernel(slots_ref, own_ref, other_ref, backward_ref, home_ref, layer_ref, input_ref):
    both_rows = home_ref.shape[1]
    rows = both_rows // 2
    for run in range(slots_ref.shape[0]):
        here = slice(run * rows, (run + 1) * rows)
        terms = home_ref[slots_ref[run]].astype(F32)
        layer_ref[here, :] = (
            own_ref[here, :] + other_ref[here, :].astype(F32) + terms[:rows]
        ).astype(layer_ref.dtype)
        input_ref[here, :] = (backward_ref[here, :] + terms[rows:]).astype(input_ref.dtype)


def ring_kernel(*refs):
    count = len(refs) // 3
    for index in range(count):
        message_ref, block_ref, out_ref = refs[2 * index], refs[2 * index + 1], refs[2 * count + index]
        out_ref[...] = (message_ref[...].astype(F32) + block_ref[...].astype(F32)).astype(
            out_ref.dtype
        )


def first_kernel(*refs):
    low_kernel(*refs[:3], refs[7])
    ring_kernel(*refs[3:7], *refs[8:])


def second_kernel(inverse_root, *refs):
    reduce_kernel(inverse_root, *refs[:5], refs[9])
    ring_kernel(*refs[5:9], *refs[10:])


def third_kernel(inverse_root, *refs):
    home_kernel(inverse_root, *refs[:7], refs[9])
    ring_kernel(*refs[7:9], refs[10])


def add_kernel(left_ref, right_ref, out_ref):
    out_ref[...] = left_ref[...] + right_ref[...]


def sum_kernel(place_ref, up_ref, down_ref, block_ref, own_ref, send_ref):
    half = place_ref[1]

    def total(index):
        return (
            up_ref[index].astype(F32)
            + down_ref[index].astype(F32)
            + block_ref[index].astype(F32)
        )

    own_ref[...] = total(half)
    send_ref[...] = total(1 - half).astype(send_ref.dtype)


def local(
    tokens,
    output_gradient,
    frozen_weight,
    adapter_down,
    adapter_up,
    down_adam_moments,
    up_adam_moments,
    feature_factors,
    rank_factors,
    run_adapter_ranks,
    run_optimizers,
    run_owner_slots,
):
    slot_count = lax.axis_size("run")
    tp_count = lax.axis_size("tp")
    ring_length = tp_count // 2
    token_rows, width = tokens.shape
    full_width = frozen_weight.shape[1]
    rank_extent = adapter_down.shape[2]
    run_count = run_adapter_ranks.shape[0]
    run_rows = token_rows // run_count
    inverse_root = 1.0 / math.sqrt(full_width)
    position = lax.axis_index("run")
    tp_self = lax.axis_index("tp")
    half_self = lax.rem(tp_self, 2)
    z_self = tp_self // 2
    place = jnp.stack(
        [position, half_self]
        + [lax.rem(z_self + offset, ring_length) for offset in range(ring_length)]
    ).astype(jnp.int32)
    run_facts = (place, run_owner_slots, run_adapter_ranks, run_optimizers)
    swap_pairs = [(index, index ^ 1) for index in range(tp_count)]
    up_pairs = [(index, (index + 2) % tp_count) for index in range(tp_count)]
    down_pairs = [(index, (index - 2) % tp_count) for index in range(tp_count)]
    z_groups = [[z * 2 + half for z in range(ring_length)] for half in range(2)]

    (to_owner,) = staged_call(
        scatter_kernel,
        (shape((slot_count, 2 * run_rows, width), BF16),),
        (run_owner_slots,),
        (tokens, output_gradient),
    )
    recv = all_to_all(to_owner, "run")

    def from_every_z(values):
        return lax.all_gather(
            values[None], "tp", axis=0, tiled=True, axis_index_groups=z_groups
        )

    grad_own = from_every_z(output_gradient)
    swapped = lax.ppermute(output_gradient, "tp", swap_pairs)
    grad_other = from_every_z(swapped)

    partial = pl.pallas_call(
        partial_kernel,
        out_shape=shape((ring_length, 2, token_rows, width), BF16),
        grid_spec=pltpu.PrefetchScalarGridSpec(
            num_scalar_prefetch=1,
            grid=(ring_length,),
            in_specs=[
                pl.BlockSpec((token_rows, width), lambda i, place: (0, 0)),
                pl.BlockSpec((width, 2 * width), lambda i, place: (0, place[2 + i])),
                pl.BlockSpec(memory_space=pl.ANY),
            ],
            out_specs=pl.BlockSpec((1, 2, token_rows, width), lambda i, place: (i, 0, 0, 0)),
        ),
        compiler_params=PARAMS,
    )(place, tokens, frozen_weight, to_owner)
    up_steps = ring_length // 2
    down_steps = ring_length - 1 - up_steps
    upward, downward = partial[up_steps], partial[ring_length - down_steps]


    def hop_up(values):
        return lax.ppermute(values, "tp", up_pairs)

    def hop_down(values):
        return lax.ppermute(values, "tp", down_pairs)

    message = shape(upward.shape, BF16)

    def ring_operands(step, upward, downward):
        operands = (hop_up(upward), (partial, up_steps - step))
        if step < down_steps:
            operands += (hop_down(downward), (partial, ring_length - down_steps + step))
        return operands

    low_part, upward, downward = staged_call(
        first_kernel,
        (
            shape((tp_count, slot_count * run_rows // tp_count, 2 * rank_extent), BF16),
            message,
            message,
        ),
        (),
        (recv, adapter_down, adapter_up) + ring_operands(1, upward, downward),
        after=(swapped,),
    )
    low_blocks = all_to_all(low_part, "tp")
    low_own, upward, downward = staged_call(
        functools.partial(second_kernel, inverse_root),
        (shape(low_blocks.shape, BF16), message, message),
        run_facts,
        (low_blocks,) + ring_operands(2, upward, downward),
    )
    low_all = all_to_all(low_own, "tp")

    to_home, upward = staged_call(
        functools.partial(third_kernel, inverse_root),
        (shape((slot_count, 2 * run_rows, width), BF16), message),
        run_facts,
        (low_all, adapter_down, adapter_up) + ring_operands(3, upward, downward),
    )
    home = all_to_all(to_home, "run")

    grad_down, grad_up, wide_new, sums = staged_call(
        functools.partial(grad_kernel, inverse_root),
        (
            shape((width, rank_extent), F32),
            shape((rank_extent, width), F32),
            shape((1, 2, width), F32),
            shape((8, rank_extent), F32),
        ),
        run_facts,
        (recv, low_all, feature_factors),
        after=(to_home,),
    )

    def sum_hop(values, hop, after=()):
        other = lax.ppermute(values, "tp", [(index, index ^ hop) for index in range(tp_count)])
        return staged_call(add_kernel, (shape(values.shape, F32),), (), (values, other), after)[0]

    sums = sum_hop(sums, 2)
    base_own, base_send = staged_call(
        sum_kernel,
        (shape((token_rows, width), F32), shape((token_rows, width), BF16)),
        (place,),
        (hop_up(upward), hop_down(downward), (partial, 0)),
        after=(sums,),
    )
    base_other = lax.ppermute(base_send, "tp", swap_pairs)
    sums = sum_hop(sums, 4, (base_send,))
    sums = sum_hop(sums, 8)

    backward_total = pl.pallas_call(
        backward_kernel,
        out_shape=shape((token_rows, width), F32),
        grid_spec=pltpu.PrefetchScalarGridSpec(
            num_scalar_prefetch=1,
            grid=(ring_length,),
            in_specs=[
                pl.BlockSpec((1, token_rows, width), lambda i, place: (i, 0, 0)),
                pl.BlockSpec((1, token_rows, width), lambda i, place: (i, 0, 0)),
                pl.BlockSpec((width, 2 * width), lambda i, place: (0, i)),
            ],
            out_specs=pl.BlockSpec((token_rows, width), lambda i, place: (0, 0)),
        ),
        compiler_params=PARAMS,
    )(place, grad_own, grad_other, frozen_weight)
    sums = sum_hop(sums, 1, (backward_total,))
    updated = staged_call(
        functools.partial(update_kernel, full_width),
        (
            shape(adapter_down.shape, BF16),
            shape(adapter_up.shape, BF16),
            shape(down_adam_moments.shape, F32),
            shape(up_adam_moments.shape, F32),
            shape(feature_factors.shape, F32),
            shape(rank_factors.shape, F32),
        ),
        run_facts,
        (
            grad_down,
            grad_up,
            wide_new,
            sums,
            adapter_down,
            adapter_up,
            down_adam_moments,
            up_adam_moments,
            feature_factors,
            rank_factors,
        ),
    )

    layer_output, input_gradient = staged_call(
        output_kernel,
        (shape((token_rows, width), BF16),) * 2,
        (run_owner_slots,),
        (base_own, base_other, backward_total, home),
        after=(updated[5],),
    )
    return (layer_output, input_gradient) + tuple(updated)


def solution(mesh):
    placed = (
        P("run", "tp"),
        P("run", "tp"),
        P("tp", None),
        P("run", "tp", None),
        P("run", None, "tp"),
        P("run", None, "tp", None),
        P("run", None, None, "tp"),
        P("run", None, "tp"),
        P("run", None, None),
        P(),
        P(),
        P(),
    )
    return jax.shard_map(
        local,
        mesh=mesh,
        in_specs=placed,
        out_specs=(
            P("run", "tp"),
            P("run", "tp"),
            P("run", "tp", None),
            P("run", None, "tp"),
            P("run", None, "tp", None),
            P("run", None, None, "tp"),
            P("run", None, "tp"),
            P("run", None, None),
        ),
        check_vma=False,
    )
```

time: 732 us -> 240 us (0.33)
  waiting for transfers between devices: 576 us -> 81.9 us
  starting transfers between devices: 28.6 us -> 88.5 us
  blocking collectives: 51.4 us -> 0 us
  Pallas kernels: 0 us -> 42.3 us
  other arithmetic: 22.7 us -> 0 us
  matrix products: 20.6 us -> 0 us
    reduce_scatter x1 -> x0, waiting for transfers between devices: 235 us -> none  [local(): lax.psum_scatter(base_term.astype(jnp.bfloat16), 'tp', scatter_dimension=...]
    psum x1 -> x0, waiting for transfers between devices: 161 us -> none  [local(): lax.psum(low_part.astype(jnp.bfloat16), 'tp').astype(jnp.float32)]
    all_gather x3 -> x2, waiting for transfers between devices: 159 us -> 0.04 us  [from_every_z(): lax.all_gather(values[None], 'tp', axis=0, tiled=True, axis_index_groups=...]
    ppermute x0 -> x13, waiting for transfers between devices: none -> 80.5 us  [the longest x4 48 us: hop_up(): return lax.ppermute(values, 'tp', up_pairs)]
    ppermute x0 -> x13, starting transfers between devices: none -> 52.2 us  [the longest x3 15.7 us: hop_down(): return lax.ppermute(values, 'tp', down_pairs)]
    psum x1 -> x0, blocking collectives: 51.4 us -> none  [local(): lax.psum((col_part, row_part, total_part), 'tp')]
    pallas_call x0 -> x14, Pallas kernels: none -> 42.3 us  [the longest x12 26.7 us: staged_call(): pl.pallas_call(without_extra, out_shape=out_shape, grid=(1,), in_specs=[S...]
    dot_general x12 -> x0, matrix products: 20.6 us -> none  [the longest x1 4.35 us: contract_last(): lax.dot_general(left_side, right_side, (((1,), (1,)), ((), ())), preferre...]
  transfers between devices with their start and end apart: 9 -> 19, of which waited for: 8 -> 10; matrix products, arithmetic and copies ran while one was open for 6% -> 1% of each run, Pallas kernels for 0% -> 17%
where the time goes in v1:
time: 240 us; the launch traced here: 238 us
  starting transfers between devices  88.5 us (37%)
  waiting for transfers between devices  81.9 us (34%)
  Pallas kernels  42.3 us (18%)
  between operations  14.4 us (6%)
  local copies, waits for them, and re-layouts  11.3 us (5%)
    ppermute x4, waiting for transfers between devices, hop_up(): return lax.ppermute(values, 'tp', up_pairs)  48 us
    all_to_all x4, starting transfers between devices, all_to_all(): return lax.all_to_all(blocks, axis, split_axis=0, concat_axis=0, tiled=True)  36.1 us
    pallas_call x12, Pallas kernels, staged_call(): pl.pallas_call(without_extra, out_shape=out_shape, grid=(1,), in_specs=[S...  26.7 us
    ppermute x4, waiting for transfers between devices, sum_hop(): lax.ppermute(values, 'tp', [(index, index ^ hop) for index in range(tp_co...  16.1 us
    ppermute x3, starting transfers between devices, hop_down(): return lax.ppermute(values, 'tp', down_pairs)  15.7 us
    ppermute x4, starting transfers between devices, sum_hop(): lax.ppermute(values, 'tp', [(index, index ^ hop) for index in range(tp_co...  15.5 us
    ppermute x1, waiting for transfers between devices, local(): swapped = lax.ppermute(output_gradient, 'tp', swap_pairs)  14.8 us
    ppermute x4, starting transfers between devices, hop_up(): return lax.ppermute(values, 'tp', up_pairs)  13.5 us
  transfers between devices with their start and end apart: 19, of which 10 were waited for; matrix products, arithmetic and copies ran while one was open for 1% of the time, Pallas kernels for 17%

profile of v1, /device:TPU:56, one launch (start us, length us, event | category | flops | bytes accessed | tf_op | source)
XLA Modules:
  0.0 238.4 jit_solution(2939067263332376007)
XLA Ops:
  7.2 0.0 all-gather.5.cloned.1.call-start
  7.2 0.7 all-gather.5.cloned.1.call-update
  7.9 2.1 shard_map.179.after_ref
  10.0 7.8 %all-to-all-start = ((bf16[32,64,256]{2,1,0:T(8,128)(2,1)}), bf16[32,64,256]{2,1,0:T(8,128)(2,1)S(1)}, u32[]{:S(2)}, u32[]{:S(2)}) async-start(bf16[32,64,256]{2,1,0:T(8,128)(2,1)} %shard_map.179.after_ref), calls=%async_computation | async-start | bytes 2097152 | tf_op jit(solution)/shard_map/all_to_all | solution.py:66
  17.9 0.7 stack.43.place_ref.refs_0_
  18.5 7.8 %shard_map.180.refs_4_.refs_6_.refs_8_.refs_3_ = bf16[8,2,512,256]{3,2,1,0:T(8,128)(2,1)} custom-call(s32[10]{0:T(128)} %stack.43.place_ref.refs_0_, bf16[512,256]{1,0:T(8,128)(2,1)} %tok_ref.1, bf16[256,4096]{1,0:T(8,128)(2,1)} %weight_ref.3, bf16[32,64,256]{2,1,0:T(8,128)(2,1)} %shard_map.179.after_ref), custom_call_target="tpu_custom_call" | custom-call | tf_op jit(solution)/shard_map/pallas_call | solution.py:417
  26.3 1.3 slice_bitcast_fusion
  27.6 4.3 %collective-permute-start = (bf16[2,512,256]{2,1,0:T(8,128)(2,1)S(1)}, bf16[2,512,256]{2,1,0:T(8,128)(2,1)S(1)}, u32[]{:S(2)}, u32[]{:S(2)}) collective-permute-start(bf16[2,512,256]{2,1,0:T(8,128)(2,1)S(1)} %get-tuple-element.53), channel_id=1, source_target_pairs={{0,2},{1,3},{2,4},{3,5},{4,6},{5,7},{6,8},{7,9},{8,10},{9,11},{10,... | collective-permute-start | bytes 1572872 | tf_op jit(solution)/shard_map/ppermute | solution.py:438
  31.9 8.6 %collective-permute-start.1 = (bf16[2,512,256]{2,1,0:T(8,128)(2,1)S(1)}, bf16[2,512,256]{2,1,0:T(8,128)(2,1)S(1)}, u32[]{:S(2)}, u32[]{:S(2)}) collective-permute-start(bf16[2,512,256]{2,1,0:T(8,128)(2,1)S(1)} %get-tuple-element.52), channel_id=1, source_target_pairs={{0,14},{1,15},{2,0},{3,1},{4,2},{5,3},{6,4},{7,5},{8,6},{9,7},{10,... | collective-permute-start | bytes 1572872 | tf_op jit(solution)/shard_map/ppermute | solution.py:441
  40.6 4.7 %collective-permute-start.2 = (bf16[512,256]{1,0:T(8,128)(2,1)S(1)}, bf16[512,256]{1,0:T(8,128)(2,1)S(1)}, u32[]{:S(2)}, u32[]{:S(2)}) collective-permute-start(bf16[512,256]{1,0:T(8,128)(2,1)S(1)} %copy-done.5), channel_id=1, source_target_pairs={{0,1},{1,0},{2,3},{3,2},{4,5},{5,4},{6,7},{7,6},{8,9},{9,8},{10,11... | collective-permute-start | bytes 786440 | tf_op jit(solution)/shard_map/ppermute | solution.py:414
  45.3 14.8 %collective-permute-done.2.refs_7_ = bf16[512,256]{1,0:T(8,128)(2,1)S(1)} collective-permute-done((bf16[512,256]{1,0:T(8,128)(2,1)S(1)}, bf16[512,256]{1,0:T(8,128)(2,1)S(1)}, u32[]{:S(2)}, u32[]{:S(2)}) %collective-permute-start.2) | collective-permute-done | bytes 262176 | tf_op jit(solution)/shard_map/ppermute | solution.py:414
  60.1 2.0 collective-permute-done.refs_3_
  62.1 0.1 collective-permute-done.1.refs_5_
  62.2 0.7 copy-done.9
  62.9 0.2 copy-done.10
  63.1 1.0 copy-done
  64.1 3.6 %shard_map.181 = (bf16[16,64,256]{2,1,0:T(8,128)(2,1)}, bf16[2,512,256]{2,1,0:T(8,128)(2,1)}, bf16[2,512,256]{2,1,0:T(8,128)(2,1)}) custom-call(bf16[32,64,256]{2,1,0:T(8,128)(2,1)} %copy-done, bf16[1,256,128]{2,1,0:T(8,128)(2,1)} %refs_8_.1, bf16[1,128,256]{2,1,0:T(8,128)(2,1)} %refs_9_.1, bf16[2,512,256]{2,1,0:T(8,128)(2,1)} %copy-done.9, ...), custom_call_target="tpu_custom_call" | custom-call | tf_op jit(solution)/shard_map/pallas_call | solution.py:44
  67.7 11.5 %all-to-all-start.1 = ((bf16[16,64,256]{2,1,0:T(8,128)(2,1)}), bf16[16,64,256]{2,1,0:T(8,128)(2,1)S(1)}, u32[]{:S(2)}, u32[]{:S(2)}) async-start(bf16[16,64,256]{2,1,0:T(8,128)(2,1)} %get-tuple-element.30), calls=%async_computation.1 | async-start | bytes 1048576 | tf_op jit(solution)/shard_map/all_to_all | solution.py:66
  79.1 0.0 all-gather.7.cloned.1.call-start
  79.2 0.7 all-gather.7.cloned.1.call-update
  79.9 3.4 %collective-permute-start.3 = (bf16[2,512,256]{2,1,0:T(8,128)(2,1)}, bf16[2,512,256]{2,1,0:T(8,128)(2,1)S(1)}, u32[]{:S(2)}, u32[]{:S(2)}) collective-permute-start(bf16[2,512,256]{2,1,0:T(8,128)(2,1)} %get-tuple-element.31), channel_id=1, source_target_pairs={{0,2},{1,3},{2,4},{3,5},{4,6},{5,7},{6,8},{7,9},{8,10},{9,11},{10,... | collective-permute-start | bytes 1572872 | tf_op jit(solution)/shard_map/ppermute | solution.py:438
  83.3 3.7 %collective-permute-start.4 = (bf16[2,512,256]{2,1,0:T(8,128)(2,1)}, bf16[2,512,256]{2,1,0:T(8,128)(2,1)S(1)}, u32[]{:S(2)}, u32[]{:S(2)}) collective-permute-start(bf16[2,512,256]{2,1,0:T(8,128)(2,1)} %get-tuple-element.32), channel_id=1, source_target_pairs={{0,14},{1,15},{2,0},{3,1},{4,2},{5,3},{6,4},{7,5},{8,6},{9,7},{10,... | collective-permute-start | bytes 1572872 | tf_op jit(solution)/shard_map/ppermute | solution.py:441
  87.0 22.5 %collective-permute-done.3.refs_5_ = bf16[2,512,256]{2,1,0:T(8,128)(2,1)S(1)} collective-permute-done((bf16[2,512,256]{2,1,0:T(8,128)(2,1)}, bf16[2,512,256]{2,1,0:T(8,128)(2,1)S(1)}, u32[]{:S(2)}, u32[]{:S(2)}) %collective-permute-start.3) | collective-permute-done | bytes 524320 | tf_op jit(solution)/shard_map/ppermute | solution.py:438
  109.4 1.5 collective-permute-done.4.refs_7_
  111.0 0.8 copy-done.12
  111.8 0.8 copy-done.3
  112.6 3.0 %shard_map.182 = (bf16[16,64,256]{2,1,0:T(8,128)(2,1)}, bf16[2,512,256]{2,1,0:T(8,128)(2,1)}, bf16[2,512,256]{2,1,0:T(8,128)(2,1)}) custom-call(s32[10]{0:T(128)} %stack.43.place_ref.refs_0_, s32[16]{0:T(128)} %refs_0_.3, s32[16]{0:T(128)} %refs_2_.11, s32[16]{0:T(128)} %refs_3_.7, bf16[16,64,256]{2,1,0:T(8,128)(2,1)} %copy-done.3, ...), custom_call_target="tpu_custom_call" | custom-call | tf_op jit(solution)/shard_map/pallas_call | solution.py:44
  115.5 9.0 %all-to-all-start.2 = ((bf16[16,64,256]{2,1,0:T(8,128)(2,1)}), bf16[16,64,256]{2,1,0:T(8,128)(2,1)S(1)}, u32[]{:S(2)}, u32[]{:S(2)}) async-start(bf16[16,64,256]{2,1,0:T(8,128)(2,1)} %get-tuple-element.33), calls=%async_computation.2 | async-start | bytes 1048576 | tf_op jit(solution)/shard_map/all_to_all | solution.py:66
  124.5 3.4 %collective-permute-start.5 = (bf16[2,512,256]{2,1,0:T(8,128)(2,1)}, bf16[2,512,256]{2,1,0:T(8,128)(2,1)S(1)}, u32[]{:S(2)}, u32[]{:S(2)}) collective-permute-start(bf16[2,512,256]{2,1,0:T(8,128)(2,1)} %get-tuple-element.34), channel_id=1, source_target_pairs={{0,2},{1,3},{2,4},{3,5},{4,6},{5,7},{6,8},{7,9},{8,10},{9,11},{10,... | collective-permute-start | bytes 1572872 | tf_op jit(solution)/shard_map/ppermute | solution.py:438
  127.9 22.4 %collective-permute-done.5.refs_7_ = bf16[2,512,256]{2,1,0:T(8,128)(2,1)S(1)} collective-permute-done((bf16[2,512,256]{2,1,0:T(8,128)(2,1)}, bf16[2,512,256]{2,1,0:T(8,128)(2,1)S(1)}, u32[]{:S(2)}, u32[]{:S(2)}) %collective-permute-start.5) | collective-permute-done | bytes 524320 | tf_op jit(solution)/shard_map/ppermute | solution.py:438
  150.2 0.0 all-to-all-done.2.refs_4_.refs_5_
  150.2 0.8 copy-done.8
  151.0 0.8 copy-done.1
  151.8 3.0 %shard_map.183 = (bf16[32,64,256]{2,1,0:T(8,128)(2,1)}, bf16[2,512,256]{2,1,0:T(8,128)(2,1)}) custom-call(s32[10]{0:T(128)} %stack.43.place_ref.refs_0_, s32[16]{0:T(128)} %refs_0_.3, s32[16]{0:T(128)} %refs_2_.11, s32[16]{0:T(128)} %refs_3_.7, bf16[16,64,256]{2,1,0:T(8,128)(2,1)} %copy-done.1, bf16[1,256,128]{2,1,0:T(8,128)(2,1)} %refs_8_.1, ...), custom_call_target="tpu_custom_call" | custom-call | tf_op jit(solution)/shard_map/pallas_call | solution.py:44
  154.9 8.0 %all-to-all-start.3 = ((bf16[32,64,256]{2,1,0:T(8,128)(2,1)}), bf16[32,64,256]{2,1,0:T(8,128)(2,1)S(1)}, u32[]{:S(2)}, u32[]{:S(2)}) async-start(bf16[32,64,256]{2,1,0:T(8,128)(2,1)} %get-tuple-element.37.refs_7_), calls=%async_computation.3 | async-start | bytes 2097152 | tf_op jit(solution)/shard_map/all_to_all | solution.py:66
  162.8 3.4 %collective-permute-start.7 = (bf16[2,512,256]{2,1,0:T(8,128)(2,1)S(1)}, bf16[2,512,256]{2,1,0:T(8,128)(2,1)S(1)}, u32[]{:S(2)}, u32[]{:S(2)}) collective-permute-start(bf16[2,512,256]{2,1,0:T(8,128)(2,1)S(1)} %copy-done.19), channel_id=1, source_target_pairs={{0,14},{1,15},{2,0},{3,1},{4,2},{5,3},{6,4},{7,5},{8,6},{9,7},{10,... | collective-permute-start | bytes 1572872 | tf_op jit(solution)/shard_map/ppermute | solution.py:441
  166.2 2.5 %collective-permute-start.6 = (bf16[2,512,256]{2,1,0:T(8,128)(2,1)S(1)}, bf16[2,512,256]{2,1,0:T(8,128)(2,1)S(1)}, u32[]{:S(2)}, u32[]{:S(2)}) collective-permute-start(bf16[2,512,256]{2,1,0:T(8,128)(2,1)S(1)} %copy-done.20), channel_id=1, source_target_pairs={{0,2},{1,3},{2,4},{3,5},{4,6},{5,7},{6,8},{7,9},{8,10},{9,11},{10,... | collective-permute-start | bytes 1572872 | tf_op jit(solution)/shard_map/ppermute | solution.py:438
  168.7 2.6 %shard_map.184 = (f32[256,128]{1,0:T(8,128)}, f32[128,256]{1,0:T(8,128)}, f32[1,2,256]{2,1,0:T(2,128)}, f32[8,128]{1,0:T(8,128)}) custom-call(s32[10]{0:T(128)} %stack.43.place_ref.refs_0_, s32[16]{0:T(128)} %refs_0_.3, s32[16]{0:T(128)} %refs_2_.11, s32[16]{0:T(128)} %refs_3_.7, bf16[32,64,256]{2,1,0:T(8,128)(2,1)} %copy-done, ...), custom_call_target="tpu_custom_call" | custom-call | tf_op jit(solution)/shard_map/pallas_call | solution.py:44
  171.3 1.9 collective-permute-start.8
  173.2 6.7 %collective-permute-done.8.refs_1_ = f32[8,128]{1,0:T(8,128)S(1)} collective-permute-done((f32[8,128]{1,0:T(8,128)}, f32[8,128]{1,0:T(8,128)S(1)}, u32[]{:S(2)}, u32[]{:S(2)}) %collective-permute-start.8) | collective-permute-done | bytes 4128 | tf_op jit(solution)/shard_map/ppermute | solution.py:493
  180.0 0.6 copy-done.17
  180.6 1.3 shard_map.185.refs_4_.refs_0_
  181.9 1.1 collective-permute-done.6.refs_1_
  183.0 0.8 copy-done.7
  183.8 2.3 shard_map.186
  186.2 2.9 %collective-permute-start.9 = (bf16[512,256]{1,0:T(8,128)(2,1)}, bf16[512,256]{1,0:T(8,128)(2,1)S(1)}, u32[]{:S(2)}, u32[]{:S(2)}) collective-permute-start(bf16[512,256]{1,0:T(8,128)(2,1)} %get-tuple-element.40.refs_2_), channel_id=1, source_target_pairs={{0,1},{1,0},{2,3},{3,2},{4,5},{5,4},{6,7},{7,6},{8,9},{9,8},{10,11... | collective-permute-start | bytes 786440 | tf_op jit(solution)/shard_map/ppermute | solution.py:504
  189.0 1.9 collective-permute-start.10
  191.0 4.4 %collective-permute-done.10.refs_1_ = f32[8,128]{1,0:T(8,128)S(1)} collective-permute-done((f32[8,128]{1,0:T(8,128)S(1)}, f32[8,128]{1,0:T(8,128)S(1)}, u32[]{:S(2)}, u32[]{:S(2)}) %collective-permute-start.10) | collective-permute-done | bytes 4128 | tf_op jit(solution)/shard_map/ppermute | solution.py:493
  195.4 0.6 copy-done.16
  196.0 1.3 shard_map.188.refs_0_
  197.3 4.7 %collective-permute-start.11 = (f32[8,128]{1,0:T(8,128)}, f32[8,128]{1,0:T(8,128)S(1)}, u32[]{:S(2)}, u32[]{:S(2)}) collective-permute-start(f32[8,128]{1,0:T(8,128)} %shard_map.188.refs_0_), channel_id=1, source_target_pairs={{0,8},{1,9},{2,10},{3,11},{4,12},{5,13},{6,14},{7,15},{8,0},{9,1},... | collective-permute-start | bytes 12296 | tf_op jit(solution)/shard_map/ppermute | solution.py:493
  202.1 4.9 %collective-permute-done.11.refs_1_ = f32[8,128]{1,0:T(8,128)S(1)} collective-permute-done((f32[8,128]{1,0:T(8,128)}, f32[8,128]{1,0:T(8,128)S(1)}, u32[]{:S(2)}, u32[]{:S(2)}) %collective-permute-start.11) | collective-permute-done | bytes 4128 | tf_op jit(solution)/shard_map/ppermute | solution.py:493
  206.9 0.6 copy-done.18
  207.5 1.3 shard_map.189.refs_0_
  208.8 6.9 %collective-permute-start.12 = (f32[8,128]{1,0:T(8,128)}, f32[8,128]{1,0:T(8,128)S(1)}, u32[]{:S(2)}, u32[]{:S(2)}) collective-permute-start(f32[8,128]{1,0:T(8,128)} %shard_map.189.refs_0_), channel_id=1, source_target_pairs={{0,1},{1,0},{2,3},{3,2},{4,5},{5,4},{6,7},{7,6},{8,9},{9,8},{10,11... | collective-permute-start | bytes 12296 | tf_op jit(solution)/shard_map/ppermute | solution.py:493
  215.7 0.0 all-gather.5.cloned.1.call-done
  215.7 0.0 all-gather.7.cloned.1.call-done
  215.7 7.8 %shard_map.187.refs_2_.refs_3_ = f32[512,256]{1,0:T(8,128)} custom-call(s32[10]{0:T(128)} %stack.43.place_ref.refs_0_, bf16[8,512,256]{2,1,0:T(8,128)(2,1)} %bitcast.16, bf16[8,512,256]{2,1,0:T(8,128)(2,1)} %bitcast.17, bf16[256,4096]{1,0:T(8,128)(2,1)} %weight_ref.3), custom_call_target="tpu_custom_call" | custom-call | tf_op jit(solution)/shard_map/pallas_call | solution.py:508
  223.6 0.6 copy-done.15
  224.2 1.3 shard_map.190.refs_7_
  225.5 2.4 shard_map.191
  227.9 0.7 copy-done.13
  228.6 0.4 copy-done.2
  229.0 2.5 %shard_map.192 = (bf16[512,256]{1,0:T(8,128)(2,1)}, bf16[512,256]{1,0:T(8,128)(2,1)}) custom-call(s32[16]{0:T(128)} %refs_0_.3, f32[512,256]{1,0:T(8,128)} %get-tuple-element.39.refs_1_, bf16[512,256]{1,0:T(8,128)(2,1)} %copy-done.13, f32[512,256]{1,0:T(8,128)} %shard_map.187.refs_2_.refs_3_, bf16[32,64,256]{2,1,0:T(8,128)(2,1)} %copy-done.2, ...), custom_call_target="tpu_custom_call" | custom-call | tf_op jit(solution)/shard_map/pallas_call | solution.py:44
  (34 shorter events, 0.1 us)
Async XLA Ops:
  7.2 208.5 %all-gather.5.cloned.1.call-start = ((), (), s32[]{:S(2)}) async-start(), calls=%async_computation.4 | async-start | bytes 2359296 | tf_op jit(solution)/shard_map/all_gather | solution.py:409
  10.0 52.2 %all-to-all-start = ((bf16[32,64,256]{2,1,0:T(8,128)(2,1)}), bf16[32,64,256]{2,1,0:T(8,128)(2,1)S(1)}, u32[]{:S(2)}, u32[]{:S(2)}) async-start(bf16[32,64,256]{2,1,0:T(8,128)(2,1)} %shard_map.179.after_ref), calls=%async_computation | async-start | bytes 2097152 | tf_op jit(solution)/shard_map/all_to_all | solution.py:66
  26.3 14.2 %copy-start.5 = (bf16[512,256]{1,0:T(8,128)(2,1)S(1)}, bf16[512,256]{1,0:T(8,128)(2,1)}, u32[]{:S(2)}) copy-start(bf16[512,256]{1,0:T(8,128)(2,1)} %refs_2_.6) | copy-start | bytes 786436
  27.6 34.5 %collective-permute-start = (bf16[2,512,256]{2,1,0:T(8,128)(2,1)S(1)}, bf16[2,512,256]{2,1,0:T(8,128)(2,1)S(1)}, u32[]{:S(2)}, u32[]{:S(2)}) collective-permute-start(bf16[2,512,256]{2,1,0:T(8,128)(2,1)S(1)} %get-tuple-element.53), channel_id=1, source_target_pairs={{0,2},{1,3},{2,4},{3,5},{4,6},{5,7},{6,8},{7,9},{8,10},{9,11},{10,... | collective-permute-start | bytes 1572872 | tf_op jit(solution)/shard_map/ppermute | solution.py:438
  31.9 30.3 %collective-permute-start.1 = (bf16[2,512,256]{2,1,0:T(8,128)(2,1)S(1)}, bf16[2,512,256]{2,1,0:T(8,128)(2,1)S(1)}, u32[]{:S(2)}, u32[]{:S(2)}) collective-permute-start(bf16[2,512,256]{2,1,0:T(8,128)(2,1)S(1)} %get-tuple-element.52), channel_id=1, source_target_pairs={{0,14},{1,15},{2,0},{3,1},{4,2},{5,3},{6,4},{7,5},{8,6},{9,7},{10,... | collective-permute-start | bytes 1572872 | tf_op jit(solution)/shard_map/ppermute | solution.py:441
  40.6 19.5 %collective-permute-start.2 = (bf16[512,256]{1,0:T(8,128)(2,1)S(1)}, bf16[512,256]{1,0:T(8,128)(2,1)S(1)}, u32[]{:S(2)}, u32[]{:S(2)}) collective-permute-start(bf16[512,256]{1,0:T(8,128)(2,1)S(1)} %copy-done.5), channel_id=1, source_target_pairs={{0,1},{1,0},{2,3},{3,2},{4,5},{5,4},{6,7},{7,6},{8,9},{9,8},{10,11... | collective-permute-start | bytes 786440 | tf_op jit(solution)/shard_map/ppermute | solution.py:414
  60.1 2.1 copy-start.4
  62.1 0.8 copy-start.9
  62.2 0.9 copy-start.10
  63.1 1.0 copy-start
  67.7 43.3 %all-to-all-start.1 = ((bf16[16,64,256]{2,1,0:T(8,128)(2,1)}), bf16[16,64,256]{2,1,0:T(8,128)(2,1)S(1)}, u32[]{:S(2)}, u32[]{:S(2)}) async-start(bf16[16,64,256]{2,1,0:T(8,128)(2,1)} %get-tuple-element.30), calls=%async_computation.1 | async-start | bytes 1048576 | tf_op jit(solution)/shard_map/all_to_all | solution.py:66
  79.1 136.6 %all-gather.7.cloned.1.call-start = ((), (), s32[]{:S(2)}) async-start(), calls=%async_computation.5 | async-start | bytes 2359296 | tf_op jit(solution)/shard_map/all_gather | solution.py:409
  79.9 29.5 %collective-permute-start.3 = (bf16[2,512,256]{2,1,0:T(8,128)(2,1)}, bf16[2,512,256]{2,1,0:T(8,128)(2,1)S(1)}, u32[]{:S(2)}, u32[]{:S(2)}) collective-permute-start(bf16[2,512,256]{2,1,0:T(8,128)(2,1)} %get-tuple-element.31), channel_id=1, source_target_pairs={{0,2},{1,3},{2,4},{3,5},{4,6},{5,7},{6,8},{7,9},{8,10},{9,11},{10,... | collective-permute-start | bytes 1572872 | tf_op jit(solution)/shard_map/ppermute | solution.py:438
  83.3 27.7 %collective-permute-start.4 = (bf16[2,512,256]{2,1,0:T(8,128)(2,1)}, bf16[2,512,256]{2,1,0:T(8,128)(2,1)S(1)}, u32[]{:S(2)}, u32[]{:S(2)}) collective-permute-start(bf16[2,512,256]{2,1,0:T(8,128)(2,1)} %get-tuple-element.32), channel_id=1, source_target_pairs={{0,14},{1,15},{2,0},{3,1},{4,2},{5,3},{6,4},{7,5},{8,6},{9,7},{10,... | collective-permute-start | bytes 1572872 | tf_op jit(solution)/shard_map/ppermute | solution.py:441
  109.4 1.6 copy-start.11
  111.0 0.8 copy-start.12
  111.8 0.8 copy-start.3
  115.5 34.7 %all-to-all-start.2 = ((bf16[16,64,256]{2,1,0:T(8,128)(2,1)}), bf16[16,64,256]{2,1,0:T(8,128)(2,1)S(1)}, u32[]{:S(2)}, u32[]{:S(2)}) async-start(bf16[16,64,256]{2,1,0:T(8,128)(2,1)} %get-tuple-element.33), calls=%async_computation.2 | async-start | bytes 1048576 | tf_op jit(solution)/shard_map/all_to_all | solution.py:66
  124.5 25.7 %collective-permute-start.5 = (bf16[2,512,256]{2,1,0:T(8,128)(2,1)}, bf16[2,512,256]{2,1,0:T(8,128)(2,1)S(1)}, u32[]{:S(2)}, u32[]{:S(2)}) collective-permute-start(bf16[2,512,256]{2,1,0:T(8,128)(2,1)} %get-tuple-element.34), channel_id=1, source_target_pairs={{0,2},{1,3},{2,4},{3,5},{4,6},{5,7},{6,8},{7,9},{8,10},{9,11},{10,... | collective-permute-start | bytes 1572872 | tf_op jit(solution)/shard_map/ppermute | solution.py:438
  150.2 0.8 copy-start.8
  151.0 0.8 copy-start.1
  154.8 8.0 %copy-start.19 = (bf16[2,512,256]{2,1,0:T(8,128)(2,1)S(1)}, bf16[2,512,256]{2,1,0:T(8,128)(2,1)}, u32[]{:S(2)}) copy-start(bf16[2,512,256]{2,1,0:T(8,128)(2,1)} %get-tuple-element.36) | copy-start | bytes 1572868
  154.8 11.4 %copy-start.20 = (bf16[2,512,256]{2,1,0:T(8,128)(2,1)S(1)}, bf16[2,512,256]{2,1,0:T(8,128)(2,1)}, u32[]{:S(2)}) copy-start(bf16[2,512,256]{2,1,0:T(8,128)(2,1)} %get-tuple-element.35) | copy-start | bytes 1572868
  154.9 73.0 %all-to-all-start.3 = ((bf16[32,64,256]{2,1,0:T(8,128)(2,1)}), bf16[32,64,256]{2,1,0:T(8,128)(2,1)S(1)}, u32[]{:S(2)}, u32[]{:S(2)}) async-start(bf16[32,64,256]{2,1,0:T(8,128)(2,1)} %get-tuple-element.37.refs_7_), calls=%async_computation.3 | async-start | bytes 2097152 | tf_op jit(solution)/shard_map/all_to_all | solution.py:66
  162.8 19.0 %collective-permute-start.7 = (bf16[2,512,256]{2,1,0:T(8,128)(2,1)S(1)}, bf16[2,512,256]{2,1,0:T(8,128)(2,1)S(1)}, u32[]{:S(2)}, u32[]{:S(2)}) collective-permute-start(bf16[2,512,256]{2,1,0:T(8,128)(2,1)S(1)} %copy-done.19), channel_id=1, source_target_pairs={{0,14},{1,15},{2,0},{3,1},{4,2},{5,3},{6,4},{7,5},{8,6},{9,7},{10,... | collective-permute-start | bytes 1572872 | tf_op jit(solution)/shard_map/ppermute | solution.py:441
  166.2 16.8 %collective-permute-start.6 = (bf16[2,512,256]{2,1,0:T(8,128)(2,1)S(1)}, bf16[2,512,256]{2,1,0:T(8,128)(2,1)S(1)}, u32[]{:S(2)}, u32[]{:S(2)}) collective-permute-start(bf16[2,512,256]{2,1,0:T(8,128)(2,1)S(1)} %copy-done.20), channel_id=1, source_target_pairs={{0,2},{1,3},{2,4},{3,5},{4,6},{5,7},{6,8},{7,9},{8,10},{9,11},{10,... | collective-permute-start | bytes 1572872 | tf_op jit(solution)/shard_map/ppermute | solution.py:438
  171.3 8.7 %collective-permute-start.8 = (f32[8,128]{1,0:T(8,128)}, f32[8,128]{1,0:T(8,128)S(1)}, u32[]{:S(2)}, u32[]{:S(2)}) collective-permute-start(f32[8,128]{1,0:T(8,128)} %get-tuple-element.38.refs_0_), channel_id=1, source_target_pairs={{0,2},{1,3},{2,0},{3,1},{4,6},{5,7},{6,4},{7,5},{8,10},{9,11},{10,... | collective-permute-start | bytes 12296 | tf_op jit(solution)/shard_map/ppermute | solution.py:493
  180.0 0.6 copy-start.17
  181.9 7.2 %copy-start.14 = (f32[8,128]{1,0:T(8,128)S(1)}, f32[8,128]{1,0:T(8,128)}, u32[]{:S(2)}) copy-start(f32[8,128]{1,0:T(8,128)} %shard_map.185.refs_4_.refs_0_) | copy-start | bytes 12292
  181.9 1.1 copy-start.6
  183.0 0.8 copy-start.7
  186.2 41.7 %collective-permute-start.9 = (bf16[512,256]{1,0:T(8,128)(2,1)}, bf16[512,256]{1,0:T(8,128)(2,1)S(1)}, u32[]{:S(2)}, u32[]{:S(2)}) collective-permute-start(bf16[512,256]{1,0:T(8,128)(2,1)} %get-tuple-element.40.refs_2_), channel_id=1, source_target_pairs={{0,1},{1,0},{2,3},{3,2},{4,5},{5,4},{6,7},{7,6},{8,9},{9,8},{10,11... | collective-permute-start | bytes 786440 | tf_op jit(solution)/shard_map/ppermute | solution.py:504
  189.0 6.4 %collective-permute-start.10 = (f32[8,128]{1,0:T(8,128)S(1)}, f32[8,128]{1,0:T(8,128)S(1)}, u32[]{:S(2)}, u32[]{:S(2)}) collective-permute-start(f32[8,128]{1,0:T(8,128)S(1)} %copy-done.14), channel_id=1, source_target_pairs={{0,4},{1,5},{2,6},{3,7},{4,0},{5,1},{6,2},{7,3},{8,12},{9,13},{10,... | collective-permute-start | bytes 12296 | tf_op jit(solution)/shard_map/ppermute | solution.py:493
  195.4 0.6 copy-start.16
  197.3 9.6 %collective-permute-start.11 = (f32[8,128]{1,0:T(8,128)}, f32[8,128]{1,0:T(8,128)S(1)}, u32[]{:S(2)}, u32[]{:S(2)}) collective-permute-start(f32[8,128]{1,0:T(8,128)} %shard_map.188.refs_0_), channel_id=1, source_target_pairs={{0,8},{1,9},{2,10},{3,11},{4,12},{5,13},{6,14},{7,15},{8,0},{9,1},... | collective-permute-start | bytes 12296 | tf_op jit(solution)/shard_map/ppermute | solution.py:493
  206.9 0.6 copy-start.18
  208.8 14.8 %collective-permute-start.12 = (f32[8,128]{1,0:T(8,128)}, f32[8,128]{1,0:T(8,128)S(1)}, u32[]{:S(2)}, u32[]{:S(2)}) collective-permute-start(f32[8,128]{1,0:T(8,128)} %shard_map.189.refs_0_), channel_id=1, source_target_pairs={{0,1},{1,0},{2,3},{3,2},{4,5},{5,4},{6,7},{7,6},{8,9},{9,8},{10,11... | collective-permute-start | bytes 12296 | tf_op jit(solution)/shard_map/ppermute | solution.py:493
  223.6 0.6 copy-start.15
  227.9 0.7 copy-start.13
  227.9 1.1 copy-start.2
Sparse Core Ops, SparseCore 0:
  10.1 56.4 all-gather.4
  82.6 49.6 all-gather.6

commit v2 on v1

--- a/solution.py
+++ b/solution.py
@@ -214,9 +214,10 @@
     row_part = to_row(jnp.sum(square_up, axis=1, keepdims=True))
     total = jnp.broadcast_to(jnp.sum(row_new, axis=1, keepdims=True), (1, extent))
     sums = jnp.concatenate(
-        [col_part, row_part, total, jnp.zeros((sums_ref.shape[0] - 3, extent), F32)], axis=0
-    )
-    sums_ref[...] = sums
+        [col_part, row_part, total, jnp.zeros((sums_ref.shape[1] - 3, extent), F32)], axis=0
+    )
+    for block in range(sums_ref.shape[0]):
+        sums_ref[block] = sums
 
 
 def update_kernel(
@@ -243,13 +244,15 @@
     new_rank_ref,
 ):
     rank, kind, holds = own_run(place_ref, slots_ref, ranks_ref, kinds_ref)
-    extent = sums_ref.shape[1]
+    extent = sums_ref.shape[2]
     is_adam = kind == 0
     held = holds == 1
     keep_row = (lax.broadcasted_iota(jnp.int32, (1, extent), 1) < rank).astype(F32)
     keep_column = (lax.broadcasted_iota(jnp.int32, (extent, 1), 0) < rank).astype(F32)
     rank_row = jnp.full((1, extent), rank, jnp.int32).astype(F32)
-    sums = sums_ref[...]
+    sums = sums_ref[0]
+    for block in range(1, sums_ref.shape[0]):
+        sums = sums + sums_ref[block]
     col_new = (
         factor_decay * rank_ref[0, 0:1, :] + (1.0 - factor_decay) * sums[0:1, :] / full_width
     ) * keep_row
@@ -325,25 +328,6 @@
         out_ref[...] = (message_ref[...].astype(F32) + block_ref[...].astype(F32)).astype(
             out_ref.dtype
         )
-
-
-def first_kernel(*refs):
-    low_kernel(*refs[:3], refs[7])
-    ring_kernel(*refs[3:7], *refs[8:])
-
-
-def second_kernel(inverse_root, *refs):
-    reduce_kernel(inverse_root, *refs[:5], refs[9])
-    ring_kernel(*refs[5:9], *refs[10:])
-
-
-def third_kernel(inverse_root, *refs):
-    home_kernel(inverse_root, *refs[:7], refs[9])
-    ring_kernel(*refs[7:9], refs[10])
-
-
-def add_kernel(left_ref, right_ref, out_ref):
-    out_ref[...] = left_ref[...] + right_ref[...]
 
 
 def sum_kernel(place_ref, up_ref, down_ref, block_ref, own_ref, send_ref):
@@ -414,24 +398,36 @@
     swapped = lax.ppermute(output_gradient, "tp", swap_pairs)
     grad_other = from_every_z(swapped)
 
-    partial = pl.pallas_call(
-        partial_kernel,
-        out_shape=shape((ring_length, 2, token_rows, width), BF16),
-        grid_spec=pltpu.PrefetchScalarGridSpec(
-            num_scalar_prefetch=1,
-            grid=(ring_length,),
-            in_specs=[
-                pl.BlockSpec((token_rows, width), lambda i, place: (0, 0)),
-                pl.BlockSpec((width, 2 * width), lambda i, place: (0, place[2 + i])),
-                pl.BlockSpec(memory_space=pl.ANY),
-            ],
-            out_specs=pl.BlockSpec((1, 2, token_rows, width), lambda i, place: (i, 0, 0, 0)),
-        ),
-        compiler_params=PARAMS,
-    )(place, tokens, frozen_weight, to_owner)
+    def partial_blocks(first, stride, count, after):
+        return pl.pallas_call(
+            partial_kernel,
+            out_shape=shape((count, 2, token_rows, width), BF16),
+            grid_spec=pltpu.PrefetchScalarGridSpec(
+                num_scalar_prefetch=1,
+                grid=(count,),
+                in_specs=[
+                    pl.BlockSpec((token_rows, width), lambda i, place: (0, 0)),
+                    pl.BlockSpec(
+                        (width, 2 * width),
+                        lambda i, place: (0, place[2 + (first + i * stride) % ring_length]),
+                    ),
+                    pl.BlockSpec(memory_space=pl.ANY),
+                ],
+                out_specs=pl.BlockSpec(
+                    (1, 2, token_rows, width), lambda i, place: (i, 0, 0, 0)
+                ),
+            ),
+            compiler_params=PARAMS,
+        )(place, tokens, frozen_weight, after)
+
     up_steps = ring_length // 2
     down_steps = ring_length - 1 - up_steps
-    upward, downward = partial[up_steps], partial[ring_length - down_steps]
+    first_blocks = partial_blocks(up_steps, 1, 2, to_owner)
+    upward, downward = first_blocks[0], first_blocks[1]
+    partial = partial_blocks(up_steps + 2, 1, ring_length - 2, first_blocks)
+
+    def block_at(offset):
+        return (partial, (offset - up_steps - 2) % ring_length)
 
 
     def hop_up(values):
@@ -443,67 +439,53 @@
     message = shape(upward.shape, BF16)
 
     def ring_operands(step, upward, downward):
-        operands = (hop_up(upward), (partial, up_steps - step))
+        operands = (hop_up(upward), block_at(up_steps - step))
         if step < down_steps:
-            operands += (hop_down(downward), (partial, ring_length - down_steps + step))
+            operands += (hop_down(downward), block_at(ring_length - down_steps + step))
         return operands
 
-    low_part, upward, downward = staged_call(
-        first_kernel,
-        (
-            shape((tp_count, slot_count * run_rows // tp_count, 2 * rank_extent), BF16),
-            message,
-            message,
-        ),
+    def ring_step(step, upward, downward, after):
+        operands = ring_operands(step, upward, downward)
+        return staged_call(
+            ring_kernel, (message,) * (len(operands) // 2), (), operands, after
+        )
+
+    upward, downward = ring_step(1, upward, downward, ())
+    (low_part,) = staged_call(
+        low_kernel,
+        (shape((tp_count, slot_count * run_rows // tp_count, 2 * rank_extent), BF16),),
         (),
-        (recv, adapter_down, adapter_up) + ring_operands(1, upward, downward),
-        after=(swapped,),
+        (recv, adapter_down, adapter_up),
+        after=(swapped, upward, downward),
     )
     low_blocks = all_to_all(low_part, "tp")
-    low_own, upward, downward = staged_call(
-        functools.partial(second_kernel, inverse_root),
-        (shape(low_blocks.shape, BF16), message, message),
+    upward, downward = ring_step(2, upward, downward, (low_part,))
+    (low_own,) = staged_call(
+        functools.partial(reduce_kernel, inverse_root),
+        (shape(low_blocks.shape, BF16),),
         run_facts,
-        (low_blocks,) + ring_operands(2, upward, downward),
+        (low_blocks,),
+        after=(upward, downward),
     )
     low_all = all_to_all(low_own, "tp")
-
-    to_home, upward = staged_call(
-        functools.partial(third_kernel, inverse_root),
-        (shape((slot_count, 2 * run_rows, width), BF16), message),
+    (upward,) = ring_step(3, upward, downward, (low_own,))
+    (to_home,) = staged_call(
+        functools.partial(home_kernel, inverse_root),
+        (shape((slot_count, 2 * run_rows, width), BF16),),
         run_facts,
-        (low_all, adapter_down, adapter_up) + ring_operands(3, upward, downward),
+        (low_all, adapter_down, adapter_up),
+        after=(upward,),
     )
     home = all_to_all(to_home, "run")
 
-    grad_down, grad_up, wide_new, sums = staged_call(
-        functools.partial(grad_kernel, inverse_root),
-        (
-            shape((width, rank_extent), F32),
-            shape((rank_extent, width), F32),
-            shape((1, 2, width), F32),
-            shape((8, rank_extent), F32),
-        ),
-        run_facts,
-        (recv, low_all, feature_factors),
-        after=(to_home,),
-    )
-
-    def sum_hop(values, hop, after=()):
-        other = lax.ppermute(values, "tp", [(index, index ^ hop) for index in range(tp_count)])
-        return staged_call(add_kernel, (shape(values.shape, F32),), (), (values, other), after)[0]
-
-    sums = sum_hop(sums, 2)
     base_own, base_send = staged_call(
         sum_kernel,
         (shape((token_rows, width), F32), shape((token_rows, width), BF16)),
         (place,),
-        (hop_up(upward), hop_down(downward), (partial, 0)),
-        after=(sums,),
+        (hop_up(upward), hop_down(downward), block_at(0)),
+        after=(to_home,),
     )
     base_other = lax.ppermute(base_send, "tp", swap_pairs)
-    sums = sum_hop(sums, 4, (base_send,))
-    sums = sum_hop(sums, 8)
 
     backward_total = pl.pallas_call(
         backward_kernel,
@@ -520,7 +502,27 @@
         ),
         compiler_params=PARAMS,
     )(place, grad_own, grad_other, frozen_weight)
-    sums = sum_hop(sums, 1, (backward_total,))
+
+    grad_down, grad_up, wide_new, sums = staged_call(
+        functools.partial(grad_kernel, inverse_root),
+        (
+            shape((width, rank_extent), F32),
+            shape((rank_extent, width), F32),
+            shape((1, 2, width), F32),
+            shape((tp_count, 8, rank_extent), F32),
+        ),
+        run_facts,
+        (recv, low_all, feature_factors),
+        after=(home, backward_total, base_other),
+    )
+    all_sums = all_to_all(sums, "tp")
+    layer_output, input_gradient = staged_call(
+        output_kernel,
+        (shape((token_rows, width), BF16),) * 2,
+        (run_owner_slots,),
+        (base_own, base_other, backward_total, home),
+        after=(sums,),
+    )
     updated = staged_call(
         functools.partial(update_kernel, full_width),
         (
@@ -536,7 +538,7 @@
             grad_down,
             grad_up,
             wide_new,
-            sums,
+            all_sums,
             adapter_down,
             adapter_up,
             down_adam_moments,
@@ -544,14 +546,7 @@
             feature_factors,
             rank_factors,
         ),
-    )
-
-    layer_output, input_gradient = staged_call(
-        output_kernel,
-        (shape((token_rows, width), BF16),) * 2,
-        (run_owner_slots,),
-        (base_own, base_other, backward_total, home),
-        after=(updated[5],),
+        after=(layer_output,),
     )
     return (layer_output, input_gradient) + tuple(updated)
 

time: 240 us -> 240 us (level)
  the two profiles are of different devices: /device:TPU:56 before, /device:TPU:10 now
where the time goes in v2:
time: 240 us; the launch traced here: 239 us
  starting transfers between devices  85.6 us (36%)
  waiting for transfers between devices  84.5 us (35%)
  Pallas kernels  43.8 us (18%)
  between operations  14.4 us (6%)
  local copies, waits for them, and re-layouts  10.4 us (4%)
    ppermute x4, waiting for transfers between devices, hop_up(): return lax.ppermute(values, 'tp', up_pairs)  57.6 us
    all_to_all x5, starting transfers between devices, all_to_all(): return lax.all_to_all(blocks, axis, split_axis=0, concat_axis=0, tiled=True)  45.1 us
    pallas_call x11, Pallas kernels, staged_call(): pl.pallas_call(without_extra, out_shape=out_shape, grid=(1,), in_specs=[S...  26.4 us
    ppermute x3, starting transfers between devices, hop_down(): return lax.ppermute(values, 'tp', down_pairs)  14.8 us
    ppermute x4, starting transfers between devices, hop_up(): return lax.ppermute(values, 'tp', up_pairs)  13.3 us
    ppermute x3, waiting for transfers between devices, hop_down(): return lax.ppermute(values, 'tp', down_pairs)  11.4 us
    all_to_all x5, waiting for transfers between devices, all_to_all(): return lax.all_to_all(blocks, axis, split_axis=0, concat_axis=0, tiled=True)  10.4 us
    pallas_call x2, Pallas kernels, partial_blocks(): pl.pallas_call(partial_kernel, out_shape=shape((count, 2, token_rows, wid...  9.51 us
  transfers between devices with their start and end apart: 16, of which 9 were waited for; matrix products, arithmetic and copies ran while one was open for 1% of the time, Pallas kernels for 16%

profile of v2, /device:TPU:10, one launch (start us, length us, event | category | flops | bytes accessed | tf_op | source)
XLA Modules:
  0.0 238.7 jit_solution(15470863763740118240)
XLA Ops:
  7.2 0.0 all-gather.5.cloned.1.call-start
  7.2 0.7 all-gather.5.cloned.1.call-update
  7.9 2.1 shard_map.179.after_ref
  10.0 9.4 %all-to-all-start = ((bf16[32,64,256]{2,1,0:T(8,128)(2,1)}), bf16[32,64,256]{2,1,0:T(8,128)(2,1)S(1)}, u32[]{:S(2)}, u32[]{:S(2)}) async-start(bf16[32,64,256]{2,1,0:T(8,128)(2,1)} %shard_map.179.after_ref), calls=%async_computation | async-start | bytes 2097152 | tf_op jit(solution)/shard_map/all_to_all | solution.py:66
  19.6 0.7 stack.43.place_ref.refs_0_
  20.2 3.1 %shard_map.180.after_ref = bf16[2,2,512,256]{3,2,1,0:T(8,128)(2,1)} custom-call(s32[10]{0:T(128)} %stack.43.place_ref.refs_0_, bf16[512,256]{1,0:T(8,128)(2,1)} %tok_ref.3, bf16[256,4096]{1,0:T(8,128)(2,1)} %weight_ref.5, bf16[32,64,256]{2,1,0:T(8,128)(2,1)} %shard_map.179.after_ref), custom_call_target="tpu_custom_call" | custom-call | tf_op jit(solution)/shard_map/pallas_call | solution.py:402
  23.4 1.3 slice_bitcast_fusion
  24.7 2.8 %collective-permute-start = (bf16[2,512,256]{2,1,0:T(8,128)(2,1)S(1)}, bf16[2,512,256]{2,1,0:T(8,128)(2,1)S(1)}, u32[]{:S(2)}, u32[]{:S(2)}) collective-permute-start(bf16[2,512,256]{2,1,0:T(8,128)(2,1)S(1)} %get-tuple-element.45), channel_id=1, source_target_pairs={{0,2},{1,3},{2,4},{3,5},{4,6},{5,7},{6,8},{7,9},{8,10},{9,11},{10,... | collective-permute-start | bytes 1572872 | tf_op jit(solution)/shard_map/ppermute | solution.py:434
  27.5 8.6 %collective-permute-start.1 = (bf16[2,512,256]{2,1,0:T(8,128)(2,1)S(1)}, bf16[2,512,256]{2,1,0:T(8,128)(2,1)S(1)}, u32[]{:S(2)}, u32[]{:S(2)}) collective-permute-start(bf16[2,512,256]{2,1,0:T(8,128)(2,1)S(1)} %get-tuple-element.44), channel_id=1, source_target_pairs={{0,14},{1,15},{2,0},{3,1},{4,2},{5,3},{6,4},{7,5},{8,6},{9,7},{10,... | collective-permute-start | bytes 1572872 | tf_op jit(solution)/shard_map/ppermute | solution.py:437
  36.1 0.0 copy-done.6
  36.1 5.0 %collective-permute-start.4 = (bf16[512,256]{1,0:T(8,128)(2,1)S(1)}, bf16[512,256]{1,0:T(8,128)(2,1)S(1)}, u32[]{:S(2)}, u32[]{:S(2)}) collective-permute-start(bf16[512,256]{1,0:T(8,128)(2,1)S(1)} %copy-done.6), channel_id=1, source_target_pairs={{0,1},{1,0},{2,3},{3,2},{4,5},{5,4},{6,7},{7,6},{8,9},{9,8},{10,11... | collective-permute-start | bytes 786440 | tf_op jit(solution)/shard_map/ppermute | solution.py:398
  41.1 6.4 %shard_map.181.refs_1_.refs_3_ = bf16[6,2,512,256]{3,2,1,0:T(8,128)(2,1)} custom-call(s32[10]{0:T(128)} %stack.43.place_ref.refs_0_, bf16[512,256]{1,0:T(8,128)(2,1)} %tok_ref.3, bf16[256,4096]{1,0:T(8,128)(2,1)} %weight_ref.5, bf16[2,2,512,256]{3,2,1,0:T(8,128)(2,1)} %shard_map.180.after_ref), custom_call_target="tpu_custom_call" | custom-call | tf_op jit(solution)/shard_map/pallas_call | solution.py:402
  47.5 10.4 %collective-permute-done.refs_0_ = bf16[2,512,256]{2,1,0:T(8,128)(2,1)S(1)} collective-permute-done((bf16[2,512,256]{2,1,0:T(8,128)(2,1)S(1)}, bf16[2,512,256]{2,1,0:T(8,128)(2,1)S(1)}, u32[]{:S(2)}, u32[]{:S(2)}) %collective-permute-start) | collective-permute-done | bytes 524320 | tf_op jit(solution)/shard_map/ppermute | solution.py:434
  57.9 0.8 collective-permute-done.1.refs_2_
  58.7 0.8 copy-done.9
  59.5 2.6 %shard_map.182 = (bf16[2,512,256]{2,1,0:T(8,128)(2,1)}, bf16[2,512,256]{2,1,0:T(8,128)(2,1)}) custom-call(bf16[2,512,256]{2,1,0:T(8,128)(2,1)} %copy-done.8, bf16[6,2,512,256]{3,2,1,0:T(8,128)(2,1)} %shard_map.181.refs_1_.refs_3_, bf16[2,512,256]{2,1,0:T(8,128)(2,1)} %copy-done.9, bf16[6,2,512,256]{3,2,1,0:T(8,128)(2,1)} %shard_map.181.refs_1_.refs_3_), custom_call_target="tpu_custom_call" | custom-call | tf_op jit(solution)/shard_map/pallas_call | solution.py:44
  62.2 0.0 collective-permute-done.4.refs_3_
  62.2 0.0 all-to-all-done.refs_0_.refs_4_
  62.2 0.7 copy-done.5
  62.9 0.4 copy-done
  63.3 2.6 %shard_map.183.refs_4_ = bf16[16,64,256]{2,1,0:T(8,128)(2,1)} custom-call(bf16[32,64,256]{2,1,0:T(8,128)(2,1)} %copy-done, bf16[1,256,128]{2,1,0:T(8,128)(2,1)} %refs_8_.1, bf16[1,128,256]{2,1,0:T(8,128)(2,1)} %refs_9_.1, bf16[512,256]{1,0:T(8,128)(2,1)} %copy-done.5, bf16[2,512,256]{2,1,0:T(8,128)(2,1)} %get-tuple-element.26.refs_4_, ...), custom_call_target="tpu_custom_call" | custom-call | tf_op jit(solution)/shard_map/pallas_call | solution.py:44
  65.9 8.2 %all-to-all-start.1 = ((bf16[16,64,256]{2,1,0:T(8,128)(2,1)}), bf16[16,64,256]{2,1,0:T(8,128)(2,1)S(1)}, u32[]{:S(2)}, u32[]{:S(2)}) async-start(bf16[16,64,256]{2,1,0:T(8,128)(2,1)} %shard_map.183.refs_4_), calls=%async_computation.1 | async-start | bytes 1048576 | tf_op jit(solution)/shard_map/all_to_all | solution.py:66
  74.1 0.0 all-gather.7.cloned.1.call-start
  74.1 0.7 all-gather.7.cloned.1.call-update
  74.8 3.8 %collective-permute-start.2 = (bf16[2,512,256]{2,1,0:T(8,128)(2,1)S(1)}, bf16[2,512,256]{2,1,0:T(8,128)(2,1)S(1)}, u32[]{:S(2)}, u32[]{:S(2)}) collective-permute-start(bf16[2,512,256]{2,1,0:T(8,128)(2,1)S(1)} %copy-done.14), channel_id=1, source_target_pairs={{0,2},{1,3},{2,4},{3,5},{4,6},{5,7},{6,8},{7,9},{8,10},{9,11},{10,... | collective-permute-start | bytes 1572872 | tf_op jit(solution)/shard_map/ppermute | solution.py:434
  78.7 3.2 %collective-permute-start.3 = (bf16[2,512,256]{2,1,0:T(8,128)(2,1)S(1)}, bf16[2,512,256]{2,1,0:T(8,128)(2,1)S(1)}, u32[]{:S(2)}, u32[]{:S(2)}) collective-permute-start(bf16[2,512,256]{2,1,0:T(8,128)(2,1)S(1)} %copy-done.13), channel_id=1, source_target_pairs={{0,14},{1,15},{2,0},{3,1},{4,2},{5,3},{6,4},{7,5},{8,6},{9,7},{10,... | collective-permute-start | bytes 1572872 | tf_op jit(solution)/shard_map/ppermute | solution.py:437
  81.9 20.4 %collective-permute-done.2.refs_0_ = bf16[2,512,256]{2,1,0:T(8,128)(2,1)S(1)} collective-permute-done((bf16[2,512,256]{2,1,0:T(8,128)(2,1)S(1)}, bf16[2,512,256]{2,1,0:T(8,128)(2,1)S(1)}, u32[]{:S(2)}, u32[]{:S(2)}) %collective-permute-start.2) | collective-permute-done | bytes 524320 | tf_op jit(solution)/shard_map/ppermute | solution.py:434
  102.3 0.5 collective-permute-done.3.refs_2_
  102.8 0.3 copy-done.17
  103.1 0.8 copy-done.18
  103.9 2.6 %shard_map.184 = (bf16[2,512,256]{2,1,0:T(8,128)(2,1)}, bf16[2,512,256]{2,1,0:T(8,128)(2,1)}) custom-call(bf16[2,512,256]{2,1,0:T(8,128)(2,1)} %copy-done.17, bf16[6,2,512,256]{3,2,1,0:T(8,128)(2,1)} %shard_map.181.refs_1_.refs_3_, bf16[2,512,256]{2,1,0:T(8,128)(2,1)} %copy-done.18, bf16[6,2,512,256]{3,2,1,0:T(8,128)(2,1)} %shard_map.181.refs_1_.refs_3_, ...), custom_call_target="tpu_custom_call" | custom-call | tf_op jit(solution)/shard_map/pallas_call | solution.py:44
  106.5 0.0 all-to-all-done.1.refs_4_
  106.5 0.8 copy-done.4
  107.3 2.0 shard_map.185.refs_2_
  109.3 10.3 %all-to-all-start.2 = ((bf16[16,64,256]{2,1,0:T(8,128)(2,1)}), bf16[16,64,256]{2,1,0:T(8,128)(2,1)S(1)}, u32[]{:S(2)}, u32[]{:S(2)}) async-start(bf16[16,64,256]{2,1,0:T(8,128)(2,1)} %shard_map.185.refs_2_), calls=%async_computation.2 | async-start | bytes 1048576 | tf_op jit(solution)/shard_map/all_to_all | solution.py:66
  119.6 3.8 %collective-permute-start.5 = (bf16[2,512,256]{2,1,0:T(8,128)(2,1)S(1)}, bf16[2,512,256]{2,1,0:T(8,128)(2,1)S(1)}, u32[]{:S(2)}, u32[]{:S(2)}) collective-permute-start(bf16[2,512,256]{2,1,0:T(8,128)(2,1)S(1)} %copy-done.11), channel_id=1, source_target_pairs={{0,2},{1,3},{2,4},{3,5},{4,6},{5,7},{6,8},{7,9},{8,10},{9,11},{10,... | collective-permute-start | bytes 1572872 | tf_op jit(solution)/shard_map/ppermute | solution.py:434
  123.4 22.8 %collective-permute-done.5.refs_0_ = bf16[2,512,256]{2,1,0:T(8,128)(2,1)S(1)} collective-permute-done((bf16[2,512,256]{2,1,0:T(8,128)(2,1)S(1)}, bf16[2,512,256]{2,1,0:T(8,128)(2,1)S(1)}, u32[]{:S(2)}, u32[]{:S(2)}) %collective-permute-start.5) | collective-permute-done | bytes 524320 | tf_op jit(solution)/shard_map/ppermute | solution.py:434
  146.3 0.8 copy-done.12
  147.1 2.1 shard_map.186.refs_7_
  149.2 0.0 all-to-all-done.2.refs_4_.refs_5_
  149.2 0.8 copy-done.2
  150.0 2.5 %shard_map.187.refs_4_ = bf16[32,64,256]{2,1,0:T(8,128)(2,1)} custom-call(s32[10]{0:T(128)} %stack.43.place_ref.refs_0_, s32[16]{0:T(128)} %refs_1_.11, s32[16]{0:T(128)} %refs_2_.11, s32[16]{0:T(128)} %refs_3_.7, bf16[16,64,256]{2,1,0:T(8,128)(2,1)} %copy-done.2, bf16[1,256,128]{2,1,0:T(8,128)(2,1)} %refs_8_.1, bf16[1,128,256]{2,1,0:T(8,128)(2,1)} %refs_9_.1, ...), custom_call_target="tpu_custom_call" | custom-call | tf_op jit(solution)/shard_map/pallas_call | solution.py:44
  152.5 8.7 %all-to-all-start.3 = ((bf16[32,64,256]{2,1,0:T(8,128)(2,1)}), bf16[32,64,256]{2,1,0:T(8,128)(2,1)S(1)}, u32[]{:S(2)}, u32[]{:S(2)}) async-start(bf16[32,64,256]{2,1,0:T(8,128)(2,1)} %shard_map.187.refs_4_), calls=%async_computation.3 | async-start | bytes 2097152 | tf_op jit(solution)/shard_map/all_to_all | solution.py:66
  161.2 3.0 %collective-permute-start.7 = (bf16[2,512,256]{2,1,0:T(8,128)(2,1)S(1)}, bf16[2,512,256]{2,1,0:T(8,128)(2,1)S(1)}, u32[]{:S(2)}, u32[]{:S(2)}) collective-permute-start(bf16[2,512,256]{2,1,0:T(8,128)(2,1)S(1)} %copy-done.10), channel_id=1, source_target_pairs={{0,14},{1,15},{2,0},{3,1},{4,2},{5,3},{6,4},{7,5},{8,6},{9,7},{10,... | collective-permute-start | bytes 1572872 | tf_op jit(solution)/shard_map/ppermute | solution.py:437
  164.2 0.0 copy-done.3
  164.3 2.8 %collective-permute-start.6 = (bf16[2,512,256]{2,1,0:T(8,128)(2,1)S(1)}, bf16[2,512,256]{2,1,0:T(8,128)(2,1)S(1)}, u32[]{:S(2)}, u32[]{:S(2)}) collective-permute-start(bf16[2,512,256]{2,1,0:T(8,128)(2,1)S(1)} %copy-done.3), channel_id=1, source_target_pairs={{0,2},{1,3},{2,4},{3,5},{4,6},{5,7},{6,8},{7,9},{8,10},{9,11},{10,... | collective-permute-start | bytes 1572872 | tf_op jit(solution)/shard_map/ppermute | solution.py:434
  167.1 10.0 %collective-permute-done.7.refs_2_ = bf16[2,512,256]{2,1,0:T(8,128)(2,1)S(1)} collective-permute-done((bf16[2,512,256]{2,1,0:T(8,128)(2,1)S(1)}, bf16[2,512,256]{2,1,0:T(8,128)(2,1)S(1)}, u32[]{:S(2)}, u32[]{:S(2)}) %collective-permute-start.7) | collective-permute-done | bytes 524320 | tf_op jit(solution)/shard_map/ppermute | solution.py:437
  177.1 4.0 %collective-permute-done.6.refs_1_ = bf16[2,512,256]{2,1,0:T(8,128)(2,1)S(1)} collective-permute-done((bf16[2,512,256]{2,1,0:T(8,128)(2,1)S(1)}, bf16[2,512,256]{2,1,0:T(8,128)(2,1)S(1)}, u32[]{:S(2)}, u32[]{:S(2)}) %collective-permute-start.6) | collective-permute-done | bytes 524320 | tf_op jit(solution)/shard_map/ppermute | solution.py:434
  181.1 0.8 copy-done.16
  181.8 2.3 shard_map.188
  184.2 7.3 %collective-permute-start.8 = (bf16[512,256]{1,0:T(8,128)(2,1)}, bf16[512,256]{1,0:T(8,128)(2,1)S(1)}, u32[]{:S(2)}, u32[]{:S(2)}) collective-permute-start(bf16[512,256]{1,0:T(8,128)(2,1)} %get-tuple-element.31), channel_id=1, source_target_pairs={{0,1},{1,0},{2,3},{3,2},{4,5},{5,4},{6,7},{7,6},{8,9},{9,8},{10,11... | collective-permute-start | bytes 786440 | tf_op jit(solution)/shard_map/ppermute | solution.py:488
  191.5 0.0 all-gather.5.cloned.1.call-done
  191.5 0.0 all-gather.7.cloned.1.call-done
  191.5 7.9 %shard_map.189.refs_8_.refs_3_ = f32[512,256]{1,0:T(8,128)} custom-call(s32[10]{0:T(128)} %stack.43.place_ref.refs_0_, bf16[8,512,256]{2,1,0:T(8,128)(2,1)} %bitcast.16, bf16[8,512,256]{2,1,0:T(8,128)(2,1)} %bitcast.17, bf16[256,4096]{1,0:T(8,128)(2,1)} %weight_ref.5), custom_call_target="tpu_custom_call" | custom-call | tf_op jit(solution)/shard_map/pallas_call | solution.py:490
  199.4 3.7 %collective-permute-done.8.refs_9_.refs_2_ = bf16[512,256]{1,0:T(8,128)(2,1)S(1)} collective-permute-done((bf16[512,256]{1,0:T(8,128)(2,1)}, bf16[512,256]{1,0:T(8,128)(2,1)S(1)}, u32[]{:S(2)}, u32[]{:S(2)}) %collective-permute-start.8) | collective-permute-done | bytes 262176 | tf_op jit(solution)/shard_map/ppermute | solution.py:488
  203.1 0.0 all-to-all-done.3.refs_7_.refs_4_
  203.1 0.7 copy-done.7
  203.8 1.0 copy-done.1
  204.7 2.6 %shard_map.190 = (f32[256,128]{1,0:T(8,128)}, f32[128,256]{1,0:T(8,128)}, f32[1,2,256]{2,1,0:T(2,128)}, f32[16,8,128]{2,1,0:T(8,128)}) custom-call(s32[10]{0:T(128)} %stack.43.place_ref.refs_0_, s32[16]{0:T(128)} %refs_1_.11, s32[16]{0:T(128)} %refs_2_.11, s32[16]{0:T(128)} %refs_3_.7, bf16[32,64,256]{2,1,0:T(8,128)(2,1)} %copy-done, ...), custom_call_target="tpu_custom_call" | custom-call | tf_op jit(solution)/shard_map/pallas_call | solution.py:44
  207.4 8.5 %all-to-all-start.4 = ((f32[16,8,128]{2,1,0:T(8,128)}), f32[16,8,128]{2,1,0:T(8,128)S(1)}, u32[]{:S(2)}, u32[]{:S(2)}) async-start(f32[16,8,128]{2,1,0:T(8,128)} %get-tuple-element.32.refs_5_), calls=%async_computation.4 | async-start | bytes 131072 | tf_op jit(solution)/shard_map/all_to_all | solution.py:66
  215.9 2.6 %shard_map.191 = (bf16[512,256]{1,0:T(8,128)(2,1)}, bf16[512,256]{1,0:T(8,128)(2,1)}) custom-call(s32[16]{0:T(128)} %refs_1_.11, f32[512,256]{1,0:T(8,128)} %get-tuple-element.30.refs_1_, bf16[512,256]{1,0:T(8,128)(2,1)} %copy-done.7, f32[512,256]{1,0:T(8,128)} %shard_map.189.refs_8_.refs_3_, bf16[32,64,256]{2,1,0:T(8,128)(2,1)} %copy-done.1, ...), custom_call_target="tpu_custom_call" | custom-call | tf_op jit(solution)/shard_map/pallas_call | solution.py:44
  218.4 10.4 %all-to-all-done.4.refs_7_ = f32[16,8,128]{2,1,0:T(8,128)S(1)} async-done(((f32[16,8,128]{2,1,0:T(8,128)}), f32[16,8,128]{2,1,0:T(8,128)S(1)}, u32[]{:S(2)}, u32[]{:S(2)}) %all-to-all-start.4) | async-done | bytes 65568 | tf_op jit(solution)/shard_map/all_to_all | solution.py:66
  228.8 0.6 copy-done.19
  229.4 2.4 shard_map.192
  (26 shorter events, 0.0 us)
Async XLA Ops:
  7.2 184.3 %all-gather.5.cloned.1.call-start = ((), (), s32[]{:S(2)}) async-start(), calls=%async_computation.5 | async-start | bytes 2359296 | tf_op jit(solution)/shard_map/all_gather | solution.py:393
  10.0 52.2 %all-to-all-start = ((bf16[32,64,256]{2,1,0:T(8,128)(2,1)}), bf16[32,64,256]{2,1,0:T(8,128)(2,1)S(1)}, u32[]{:S(2)}, u32[]{:S(2)}) async-start(bf16[32,64,256]{2,1,0:T(8,128)(2,1)} %shard_map.179.after_ref), calls=%async_computation | async-start | bytes 2097152 | tf_op jit(solution)/shard_map/all_to_all | solution.py:66
  23.4 12.7 %copy-start.6 = (bf16[512,256]{1,0:T(8,128)(2,1)S(1)}, bf16[512,256]{1,0:T(8,128)(2,1)}, u32[]{:S(2)}) copy-start(bf16[512,256]{1,0:T(8,128)(2,1)} %refs_2_.6) | copy-start | bytes 786436
  24.7 33.2 %collective-permute-start = (bf16[2,512,256]{2,1,0:T(8,128)(2,1)S(1)}, bf16[2,512,256]{2,1,0:T(8,128)(2,1)S(1)}, u32[]{:S(2)}, u32[]{:S(2)}) collective-permute-start(bf16[2,512,256]{2,1,0:T(8,128)(2,1)S(1)} %get-tuple-element.45), channel_id=1, source_target_pairs={{0,2},{1,3},{2,4},{3,5},{4,6},{5,7},{6,8},{7,9},{8,10},{9,11},{10,... | collective-permute-start | bytes 1572872 | tf_op jit(solution)/shard_map/ppermute | solution.py:434
  27.5 31.3 %collective-permute-start.1 = (bf16[2,512,256]{2,1,0:T(8,128)(2,1)S(1)}, bf16[2,512,256]{2,1,0:T(8,128)(2,1)S(1)}, u32[]{:S(2)}, u32[]{:S(2)}) collective-permute-start(bf16[2,512,256]{2,1,0:T(8,128)(2,1)S(1)} %get-tuple-element.44), channel_id=1, source_target_pairs={{0,14},{1,15},{2,0},{3,1},{4,2},{5,3},{6,4},{7,5},{8,6},{9,7},{10,... | collective-permute-start | bytes 1572872 | tf_op jit(solution)/shard_map/ppermute | solution.py:437
  36.1 26.1 %collective-permute-start.4 = (bf16[512,256]{1,0:T(8,128)(2,1)S(1)}, bf16[512,256]{1,0:T(8,128)(2,1)S(1)}, u32[]{:S(2)}, u32[]{:S(2)}) collective-permute-start(bf16[512,256]{1,0:T(8,128)(2,1)S(1)} %copy-done.6), channel_id=1, source_target_pairs={{0,1},{1,0},{2,3},{3,2},{4,5},{5,4},{6,7},{7,6},{8,9},{9,8},{10,11... | collective-permute-start | bytes 786440 | tf_op jit(solution)/shard_map/ppermute | solution.py:398
  57.9 0.9 copy-start.8
  58.7 0.8 copy-start.9
  62.2 0.7 copy-start.5
  62.2 1.1 copy-start
  63.3 11.5 %copy-start.14 = (bf16[2,512,256]{2,1,0:T(8,128)(2,1)S(1)}, bf16[2,512,256]{2,1,0:T(8,128)(2,1)}, u32[]{:S(2)}) copy-start(bf16[2,512,256]{2,1,0:T(8,128)(2,1)} %get-tuple-element.26.refs_4_) | copy-start | bytes 1572868
  63.3 15.4 %copy-start.13 = (bf16[2,512,256]{2,1,0:T(8,128)(2,1)S(1)}, bf16[2,512,256]{2,1,0:T(8,128)(2,1)}, u32[]{:S(2)}) copy-start(bf16[2,512,256]{2,1,0:T(8,128)(2,1)} %get-tuple-element.27.refs_5_) | copy-start | bytes 1572868
  65.9 40.6 %all-to-all-start.1 = ((bf16[16,64,256]{2,1,0:T(8,128)(2,1)}), bf16[16,64,256]{2,1,0:T(8,128)(2,1)S(1)}, u32[]{:S(2)}, u32[]{:S(2)}) async-start(bf16[16,64,256]{2,1,0:T(8,128)(2,1)} %shard_map.183.refs_4_), calls=%async_computation.1 | async-start | bytes 1048576 | tf_op jit(solution)/shard_map/all_to_all | solution.py:66
  74.1 117.4 %all-gather.7.cloned.1.call-start = ((), (), s32[]{:S(2)}) async-start(), calls=%async_computation.6 | async-start | bytes 2359296 | tf_op jit(solution)/shard_map/all_gather | solution.py:393
  74.8 27.5 %collective-permute-start.2 = (bf16[2,512,256]{2,1,0:T(8,128)(2,1)S(1)}, bf16[2,512,256]{2,1,0:T(8,128)(2,1)S(1)}, u32[]{:S(2)}, u32[]{:S(2)}) collective-permute-start(bf16[2,512,256]{2,1,0:T(8,128)(2,1)S(1)} %copy-done.14), channel_id=1, source_target_pairs={{0,2},{1,3},{2,4},{3,5},{4,6},{5,7},{6,8},{7,9},{8,10},{9,11},{10,... | collective-permute-start | bytes 1572872 | tf_op jit(solution)/shard_map/ppermute | solution.py:434
  78.7 24.2 %collective-permute-start.3 = (bf16[2,512,256]{2,1,0:T(8,128)(2,1)S(1)}, bf16[2,512,256]{2,1,0:T(8,128)(2,1)S(1)}, u32[]{:S(2)}, u32[]{:S(2)}) collective-permute-start(bf16[2,512,256]{2,1,0:T(8,128)(2,1)S(1)} %copy-done.13), channel_id=1, source_target_pairs={{0,14},{1,15},{2,0},{3,1},{4,2},{5,3},{6,4},{7,5},{8,6},{9,7},{10,... | collective-permute-start | bytes 1572872 | tf_op jit(solution)/shard_map/ppermute | solution.py:437
  102.3 0.8 copy-start.17
  103.1 0.8 copy-start.18
  106.5 13.1 %copy-start.11 = (bf16[2,512,256]{2,1,0:T(8,128)(2,1)S(1)}, bf16[2,512,256]{2,1,0:T(8,128)(2,1)}, u32[]{:S(2)}) copy-start(bf16[2,512,256]{2,1,0:T(8,128)(2,1)} %get-tuple-element.28.refs_5_) | copy-start | bytes 1572868
  106.5 0.8 copy-start.4
  109.3 39.9 %all-to-all-start.2 = ((bf16[16,64,256]{2,1,0:T(8,128)(2,1)}), bf16[16,64,256]{2,1,0:T(8,128)(2,1)S(1)}, u32[]{:S(2)}, u32[]{:S(2)}) async-start(bf16[16,64,256]{2,1,0:T(8,128)(2,1)} %shard_map.185.refs_2_), calls=%async_computation.2 | async-start | bytes 1048576 | tf_op jit(solution)/shard_map/all_to_all | solution.py:66
  119.6 26.7 %collective-permute-start.5 = (bf16[2,512,256]{2,1,0:T(8,128)(2,1)S(1)}, bf16[2,512,256]{2,1,0:T(8,128)(2,1)S(1)}, u32[]{:S(2)}, u32[]{:S(2)}) collective-permute-start(bf16[2,512,256]{2,1,0:T(8,128)(2,1)S(1)} %copy-done.11), channel_id=1, source_target_pairs={{0,2},{1,3},{2,4},{3,5},{4,6},{5,7},{6,8},{7,9},{8,10},{9,11},{10,... | collective-permute-start | bytes 1572872 | tf_op jit(solution)/shard_map/ppermute | solution.py:434
  146.3 0.8 copy-start.12
  149.2 12.0 %copy-start.10 = (bf16[2,512,256]{2,1,0:T(8,128)(2,1)S(1)}, bf16[2,512,256]{2,1,0:T(8,128)(2,1)}, u32[]{:S(2)}) copy-start(bf16[2,512,256]{2,1,0:T(8,128)(2,1)} %get-tuple-element.29.refs_6_) | copy-start | bytes 1572868
  149.2 15.1 %copy-start.3 = (bf16[2,512,256]{2,1,0:T(8,128)(2,1)S(1)}, bf16[2,512,256]{2,1,0:T(8,128)(2,1)}, u32[]{:S(2)}) copy-start(bf16[2,512,256]{2,1,0:T(8,128)(2,1)} %shard_map.186.refs_7_) | copy-start | bytes 1572868
  149.2 0.8 copy-start.2
  152.5 50.6 %all-to-all-start.3 = ((bf16[32,64,256]{2,1,0:T(8,128)(2,1)}), bf16[32,64,256]{2,1,0:T(8,128)(2,1)S(1)}, u32[]{:S(2)}, u32[]{:S(2)}) async-start(bf16[32,64,256]{2,1,0:T(8,128)(2,1)} %shard_map.187.refs_4_), calls=%async_computation.3 | async-start | bytes 2097152 | tf_op jit(solution)/shard_map/all_to_all | solution.py:66
  161.2 15.9 %collective-permute-start.7 = (bf16[2,512,256]{2,1,0:T(8,128)(2,1)S(1)}, bf16[2,512,256]{2,1,0:T(8,128)(2,1)S(1)}, u32[]{:S(2)}, u32[]{:S(2)}) collective-permute-start(bf16[2,512,256]{2,1,0:T(8,128)(2,1)S(1)} %copy-done.10), channel_id=1, source_target_pairs={{0,14},{1,15},{2,0},{3,1},{4,2},{5,3},{6,4},{7,5},{8,6},{9,7},{10,... | collective-permute-start | bytes 1572872 | tf_op jit(solution)/shard_map/ppermute | solution.py:437
  164.3 16.8 %collective-permute-start.6 = (bf16[2,512,256]{2,1,0:T(8,128)(2,1)S(1)}, bf16[2,512,256]{2,1,0:T(8,128)(2,1)S(1)}, u32[]{:S(2)}, u32[]{:S(2)}) collective-permute-start(bf16[2,512,256]{2,1,0:T(8,128)(2,1)S(1)} %copy-done.3), channel_id=1, source_target_pairs={{0,2},{1,3},{2,4},{3,5},{4,6},{5,7},{6,8},{7,9},{8,10},{9,11},{10,... | collective-permute-start | bytes 1572872 | tf_op jit(solution)/shard_map/ppermute | solution.py:434
  177.1 4.0 %copy-start.15 = (bf16[2,512,256]{2,1,0:T(8,128)(2,1)}, bf16[2,512,256]{2,1,0:T(8,128)(2,1)S(1)}, u32[]{:S(2)}) copy-start(bf16[2,512,256]{2,1,0:T(8,128)(2,1)S(1)} %collective-permute-done.7.refs_2_) | copy-start | bytes 1572868
  181.1 0.8 copy-start.16
  184.2 18.9 %collective-permute-start.8 = (bf16[512,256]{1,0:T(8,128)(2,1)}, bf16[512,256]{1,0:T(8,128)(2,1)S(1)}, u32[]{:S(2)}, u32[]{:S(2)}) collective-permute-start(bf16[512,256]{1,0:T(8,128)(2,1)} %get-tuple-element.31), channel_id=1, source_target_pairs={{0,1},{1,0},{2,3},{3,2},{4,5},{5,4},{6,7},{7,6},{8,9},{9,8},{10,11... | collective-permute-start | bytes 786440 | tf_op jit(solution)/shard_map/ppermute | solution.py:488
  203.1 0.7 copy-start.7
  203.8 1.0 copy-start.1
  207.4 21.4 %all-to-all-start.4 = ((f32[16,8,128]{2,1,0:T(8,128)}), f32[16,8,128]{2,1,0:T(8,128)S(1)}, u32[]{:S(2)}, u32[]{:S(2)}) async-start(f32[16,8,128]{2,1,0:T(8,128)} %get-tuple-element.32.refs_5_), calls=%async_computation.4 | async-start | bytes 131072 | tf_op jit(solution)/shard_map/all_to_all | solution.py:66
  228.8 0.6 copy-start.19
Sparse Core Ops, SparseCore 0:
  10.1 56.4 all-gather.4
  77.6 51.7 all-gather.6
